TPU v7x, 32 devices: a whole 2x2x4 slice. The times are simulated.
32 devices in a mesh: ctx: 32 (over z, y, x, core).
Axes of the slice: x: 2, y: 2, z: 4, core: 2. Of those that a mesh axis runs over, the one named last changes fastest.
Arguments:
- hidden_in: bfloat16 [16384, 768], P('ctx'), may hold values from -12 to 12
- block_pairs: int32 [32], replicated, may hold values from 0 to 15, as said below
- ln1_gain: bfloat16 [768], P('ctx'), may hold values from 0.5 to 1.5
- ln1_bias: bfloat16 [768], P('ctx'), may hold values from -1.25 to 1.25
- qkv_weight: bfloat16 [768, 2304], P('ctx'), may hold values from -0.21875 to 0.21875
- query_bias: bfloat16 [768], P('ctx'), may hold values from -1.25 to 1.25
- value_bias: bfloat16 [768], P('ctx'), may hold values from -1.25 to 1.25
- out_weight: bfloat16 [768, 768], P('ctx'), may hold values from -2.5 to 2.5
- out_bias: bfloat16 [768], P('ctx'), may hold values from -1.25 to 1.25
- ln2_gain: bfloat16 [768], P('ctx'), may hold values from 0.5 to 1.5
- ln2_bias: bfloat16 [768], P('ctx'), may hold values from -1.25 to 1.25
- fc_weight: bfloat16 [768, 3072], P('ctx'), may hold values from -0.21875 to 0.21875
- fc_bias: bfloat16 [3072], P('ctx'), may hold values from -1.25 to 1.25
- proj_weight: bfloat16 [3072, 768], P('ctx'), may hold values from -0.109375 to 0.109375
- proj_bias: bfloat16 [768], P('ctx'), may hold values from -1.25 to 1.25
- out_grad: bfloat16 [16384, 768], P('ctx'), may hold values from -12 to 12
Outputs:
- layer_out: bfloat16 [16384, 768], P('ctx')
- grad_hidden: bfloat16 [16384, 768], P('ctx')
- grad_ln1_gain: float32 [768], P('ctx')
- grad_ln1_bias: float32 [768], P('ctx')
- grad_qkv_weight: float32 [768, 2304], P('ctx')
- grad_query_bias: float32 [768], P('ctx')
- grad_value_bias: float32 [768], P('ctx')
- grad_out_weight: float32 [768, 768], P('ctx')
- grad_out_bias: float32 [768], P('ctx')
- grad_ln2_gain: float32 [768], P('ctx')
- grad_ln2_bias: float32 [768], P('ctx')
- grad_fc_weight: float32 [768, 3072], P('ctx')
- grad_fc_bias: float32 [3072], P('ctx')
- grad_proj_weight: float32 [3072, 768], P('ctx')
- grad_proj_bias: float32 [768], P('ctx')
Inputs may be any that keep to these rules, and one draw needn't show every extreme that they name: `block_pairs`: entries 2 i and 2 i + 1 are equal, and each number of 0 to 15 appears exactly twice.
All inputs are finite; a program needn't handle non-finite values.
Results may differ from a plain program's by a relative error of at most 0.02.
Values may be sent and summed in bfloat16 or wider, within the bound.
A program may use at most 768 MiB of HBM per device.

v0:
```python
from functools import partial
import math

import jax
import jax.numpy as jnp
from jax import lax
from jax.sharding import PartitionSpec as P

HEADS = 12
SEQS = 4


NEG = -1e30


def from_partner(value, axis, bit):
    return lax.ppermute(value, axis, [(i, i ^ 1 << bit) for i in range(lax.axis_size(axis))])


def layer_norm(values, gain, bias):
    center = values - jnp.mean(values, axis=-1, keepdims=True)
    spread_sq = jnp.mean(center * center, axis=-1, keepdims=True)
    return center * lax.rsqrt(spread_sq + 1e-05) * gain + bias


def gelu_tanh(values):
    return jax.nn.gelu(values, approximate=True)


def heads_of(tensor, head_count):
    return tensor.reshape(tensor.shape[:-1] + (head_count, tensor.shape[-1] // head_count))


def pick_own(owned, chosen):
    selector = chosen.reshape((1, -1) + (1,) * (owned.ndim - 2))
    return jnp.where(selector, owned[:, 0:1], owned[:, 1:2])


def pick_piece(piece, chosen):
    selector = chosen.reshape((1, -1) + (1,) * (piece.ndim - 3))
    return jnp.where(selector, piece[:, 0], piece[:, 1])


def parity_masks(chosen, usable):
    return jnp.stack([chosen & usable, jnp.logical_not(chosen) & usable])


def spread(values, parity):
    shaped = parity.reshape((1,) + parity.shape + (1,) * (values.ndim - 2))
    return jnp.sum(jnp.where(shaped, values[:, None], 0.0), axis=2)


def group_loop(pieces, unit_rows, table, stepper, carried):
    piece_rows = pieces[0].shape[2]
    group_size = min(unit_rows, piece_rows)
    group_count = piece_rows // group_size
    batch_groups = math.gcd(group_count, max(1, 1024 // group_size))
    turn_count = group_count // batch_groups
    shaped = tuple(
        (
            item.reshape(item.shape[:2] + (group_count, group_size) + item.shape[3:])
            for item in pieces
        )
    )
    device_ids = jnp.arange(group_count, dtype=jnp.int32) * group_size // unit_rows
    table_size = table.shape[0]
    blocks = jnp.sum(
        jnp.where(
            device_ids[:, None] == jnp.arange(table_size, dtype=jnp.int32)[None, :],
            table[None, :],
            0,
        ),
        axis=1,
    )

    def one_turn(position, current):
        pieces_now = tuple(
            (
                lax.dynamic_slice_in_dim(item, position * batch_groups, batch_groups, 2)
                for item in shaped
            )
        )
        chosen = lax.dynamic_slice_in_dim(blocks, position * batch_groups, batch_groups, 0)
        return stepper(current, pieces_now, chosen)

    return lax.fori_loop(0, turn_count, one_turn, carried)


def attend_step(q_heads, my_block, score_scale, head_count, carried, pieces_now, chosen):
    key_piece = heads_of(pieces_now[0], head_count)
    value_piece = heads_of(pieces_now[1], head_count)
    earlier = chosen < my_block
    usable = chosen != my_block
    parity = parity_masks(earlier, usable)
    query_sel = pick_own(q_heads, earlier)
    key_sel = pick_piece(key_piece, earlier)
    value_sel = pick_piece(value_piece, earlier)
    scores = (
        jnp.einsum("jgqhe,jgkhe->jghqk", query_sel, key_sel, preferred_element_type=jnp.float32)
        * score_scale
    )
    usable_mask = usable.reshape(1, -1, 1, 1, 1)
    scores = jnp.where(usable_mask, scores, NEG)
    old_max, old_total, old_sum = carried
    group_max = jnp.max(scores, axis=-1)
    candidate = jnp.max(jnp.where(parity.reshape(1, 2, -1, 1, 1), group_max[:, None], NEG), axis=2)
    new_max = jnp.maximum(old_max, candidate)
    max_sel = pick_own(new_max, earlier)
    weights_exp = jnp.where(usable_mask, jnp.exp(scores - max_sel[..., None]), 0.0)
    moved = jnp.einsum(
        "jghqk,jgkhe->jgqhe",
        weights_exp.astype(jnp.bfloat16),
        value_sel,
        preferred_element_type=jnp.float32,
    )
    factor = jnp.exp(old_max - new_max)
    new_total = old_total * factor + spread(jnp.sum(weights_exp, axis=-1), parity)
    new_sum = old_sum * jnp.swapaxes(factor, 2, 3)[..., None] + spread(moved, parity)
    return (new_max, new_total, new_sum)


def query_grad_step(
    q_heads,
    grad_heads,
    lse_heads,
    delta_heads,
    my_block,
    score_scale,
    head_count,
    carried,
    pieces_now,
    chosen,
):
    key_piece = heads_of(pieces_now[0], head_count)
    value_piece = heads_of(pieces_now[1], head_count)
    earlier = chosen < my_block
    usable = chosen != my_block
    parity = parity_masks(earlier, usable)
    query_sel = pick_own(q_heads, earlier)
    grad_sel = pick_own(grad_heads, earlier)
    lse_sel = pick_own(lse_heads, earlier)
    delta_sel = pick_own(delta_heads, earlier)
    key_sel = pick_piece(key_piece, earlier)
    value_sel = pick_piece(value_piece, earlier)
    scores = (
        jnp.einsum("jgqhe,jgkhe->jghqk", query_sel, key_sel, preferred_element_type=jnp.float32)
        * score_scale
    )
    usable_mask = usable.reshape(1, -1, 1, 1, 1)
    probabilities = jnp.where(usable_mask, jnp.exp(scores - lse_sel[..., None]), 0.0)
    grad_probs = jnp.einsum(
        "jgqhe,jgkhe->jghqk", grad_sel, value_sel, preferred_element_type=jnp.float32
    )
    grad_scores = (probabilities * (grad_probs - delta_sel[..., None])).astype(jnp.bfloat16)
    term = (
        jnp.einsum("jghqk,jgkhe->jgqhe", grad_scores, key_sel, preferred_element_type=jnp.float32)
        * score_scale
    )
    return carried + spread(term, parity)


def key_grad_step(k_heads, v_heads, my_block, score_scale, head_count, carried, pieces_now, chosen):
    query_piece = heads_of(pieces_now[0], head_count)
    grad_piece = heads_of(pieces_now[1], head_count)
    later = my_block < chosen
    usable = chosen != my_block
    parity = parity_masks(later, usable)
    query_sel = pick_piece(query_piece, later)
    grad_sel = pick_piece(grad_piece, later)
    lse_sel = jnp.swapaxes(pick_piece(pieces_now[2], later), 2, 3)
    delta_sel = jnp.swapaxes(pick_piece(pieces_now[3], later), 2, 3)
    key_sel = pick_own(k_heads, later)
    value_sel = pick_own(v_heads, later)
    scores = (
        jnp.einsum("jgqhe,jgkhe->jghqk", query_sel, key_sel, preferred_element_type=jnp.float32)
        * score_scale
    )
    usable_mask = usable.reshape(1, -1, 1, 1, 1)
    probabilities = jnp.where(usable_mask, jnp.exp(scores - lse_sel[..., None]), 0.0)
    grad_probs = jnp.einsum(
        "jgqhe,jgkhe->jghqk", grad_sel, value_sel, preferred_element_type=jnp.float32
    )
    grad_scores = (probabilities * (grad_probs - delta_sel[..., None])).astype(jnp.bfloat16)
    key_term = (
        jnp.einsum("jghqk,jgqhe->jgkhe", grad_scores, query_sel, preferred_element_type=jnp.float32)
        * score_scale
    )
    value_term = jnp.einsum(
        "jghqk,jgqhe->jgkhe",
        probabilities.astype(jnp.bfloat16),
        grad_sel,
        preferred_element_type=jnp.float32,
    )
    return (carried[0] + spread(key_term, parity), carried[1] + spread(value_term, parity))


def shards(
    hidden_in,
    block_pairs,
    ln1_gain,
    ln1_bias,
    qkv_weight,
    query_bias,
    value_bias,
    out_weight,
    out_bias,
    ln2_gain,
    ln2_bias,
    fc_weight,
    fc_bias,
    proj_weight,
    proj_bias,
    out_grad,
):
    params = (
        ln1_gain,
        ln1_bias,
        qkv_weight,
        query_bias,
        value_bias,
        out_weight,
        out_bias,
        ln2_gain,
        ln2_bias,
        fc_weight,
        fc_bias,
        proj_weight,
        proj_bias,
    )
    gathered = (
        lax.all_gather(params[0], "ctx", axis=0, tiled=True),
        lax.all_gather(params[1], "ctx", axis=0, tiled=True),
        lax.all_gather(params[2], "ctx", axis=0, tiled=True),
        lax.all_gather(params[3], "ctx", axis=0, tiled=True),
        lax.all_gather(params[4], "ctx", axis=0, tiled=True),
        lax.all_gather(params[5], "ctx", axis=0, tiled=True),
        lax.all_gather(params[6], "ctx", axis=0, tiled=True),
        lax.all_gather(params[7], "ctx", axis=0, tiled=True),
        lax.all_gather(params[8], "ctx", axis=0, tiled=True),
        lax.all_gather(params[9], "ctx", axis=0, tiled=True),
        lax.all_gather(params[10], "ctx", axis=0, tiled=True),
        lax.all_gather(params[11], "ctx", axis=0, tiled=True),
        lax.all_gather(params[12], "ctx", axis=0, tiled=True),
    )
    (
        gain_one,
        bias_one,
        w_qkv,
        b_query,
        b_value,
        w_out,
        b_out,
        gain_two,
        bias_two,
        w_fc,
        b_fc,
        w_proj,
        b_proj,
    ) = gathered
    device = lax.axis_index("ctx")
    partner = device + 1 - 2 * (device % 2)
    row_count = hidden_in.shape[0]
    model_width = hidden_in.shape[1]
    unit_rows = row_count // SEQS
    halves = SEQS // 2
    head_count = HEADS
    head_size = model_width // head_count
    score_scale = 1.0 / math.sqrt(head_size)
    my_block = block_pairs[device]
    seq_shape = (halves, 2, unit_rows, model_width)
    head_shape = (halves, 2, unit_rows, head_count, head_size)
    inputs = hidden_in.astype(jnp.float32)
    normed = layer_norm(inputs, gain_one.astype(jnp.float32), bias_one.astype(jnp.float32)).astype(
        jnp.bfloat16
    )
    mixed_proj = jnp.dot(normed, w_qkv, preferred_element_type=jnp.float32)
    queries = (mixed_proj[:, :model_width] + b_query.astype(jnp.float32)).astype(jnp.bfloat16)
    key_rows = mixed_proj[:, model_width : 2 * model_width].astype(jnp.bfloat16)
    value_rows = (mixed_proj[:, 2 * model_width :] + b_value.astype(jnp.float32)).astype(
        jnp.bfloat16
    )
    q_seq = queries.reshape(seq_shape)
    k_seq = key_rows.reshape(seq_shape)
    v_seq = value_rows.reshape(seq_shape)
    q_heads = queries.reshape(head_shape)
    k_heads = key_rows.reshape(head_shape)
    v_heads = value_rows.reshape(head_shape)
    far_keys, far_values = from_partner((k_seq, v_seq), "ctx", 0)
    near_keys = jnp.concatenate([k_heads, heads_of(far_keys, head_count)], axis=2)
    near_values = jnp.concatenate([v_heads, heads_of(far_values, head_count)], axis=2)
    scores = (
        jnp.einsum("jpqhe,jpkhe->jphqk", q_heads, near_keys, preferred_element_type=jnp.float32)
        * score_scale
    )
    row_max = jnp.max(scores, axis=-1)
    weights_exp = jnp.exp(scores - row_max[..., None])
    row_total = jnp.sum(weights_exp, axis=-1)
    summed = jnp.einsum(
        "jphqk,jpkhe->jpqhe",
        weights_exp.astype(jnp.bfloat16),
        near_values,
        preferred_element_type=jnp.float32,
    )
    forward_stepper = partial(attend_step, q_heads, my_block, score_scale, head_count)
    row_max, row_total, summed = group_loop(
        (
            lax.all_gather(k_seq, "ctx", axis=2, tiled=True),
            lax.all_gather(v_seq, "ctx", axis=2, tiled=True),
        ),
        unit_rows,
        block_pairs,
        forward_stepper,
        (row_max, row_total, summed),
    )
    attended = summed / jnp.swapaxes(row_total, 2, 3)[..., None]
    log_total = row_max + jnp.log(row_total)
    att_low = attended.reshape(row_count, model_width).astype(jnp.bfloat16)
    branch = jnp.dot(att_low, w_out, preferred_element_type=jnp.float32) + b_out.astype(jnp.float32)
    middle = inputs + branch
    normed_two = layer_norm(
        middle, gain_two.astype(jnp.float32), bias_two.astype(jnp.float32)
    ).astype(jnp.bfloat16)
    pre_act = jnp.dot(normed_two, w_fc, preferred_element_type=jnp.float32) + b_fc.astype(
        jnp.float32
    )
    activation = gelu_tanh(pre_act).astype(jnp.bfloat16)
    result = (
        middle
        + jnp.dot(activation, w_proj, preferred_element_type=jnp.float32)
        + b_proj.astype(jnp.float32)
    )
    layer_out = result.astype(jnp.bfloat16)
    grad_out = out_grad.astype(jnp.float32)
    grad_proj = jnp.dot(activation.T, out_grad, preferred_element_type=jnp.float32)
    grad_bproj = jnp.sum(grad_out, axis=0)
    grad_activ = jnp.dot(out_grad, w_proj.T, preferred_element_type=jnp.float32)
    _, gelu_back = jax.vjp(gelu_tanh, pre_act)
    grad_pre = gelu_back(grad_activ)[0].astype(jnp.bfloat16)
    grad_fc = jnp.dot(normed_two.T, grad_pre, preferred_element_type=jnp.float32)
    grad_bfc = jnp.sum(grad_pre.astype(jnp.float32), axis=0)
    grad_normed_two = jnp.dot(grad_pre, w_fc.T, preferred_element_type=jnp.float32)
    _, norm_back_two = jax.vjp(
        layer_norm, middle, gain_two.astype(jnp.float32), bias_two.astype(jnp.float32)
    )
    grad_middle, grad_gain_two, grad_bias_two = norm_back_two(grad_normed_two)
    grad_middle = grad_middle + grad_out
    grad_branch = grad_middle.astype(jnp.bfloat16)
    grad_wout = jnp.dot(att_low.T, grad_branch, preferred_element_type=jnp.float32)
    grad_bout = jnp.sum(grad_branch.astype(jnp.float32), axis=0)
    grad_att = jnp.dot(grad_branch, w_out.T, preferred_element_type=jnp.float32).astype(
        jnp.bfloat16
    )
    grad_seq = grad_att.reshape(seq_shape)
    grad_heads = grad_att.reshape(head_shape)
    row_delta = jnp.sum(grad_heads.astype(jnp.float32) * attended, axis=-1)
    delta_heads = jnp.swapaxes(row_delta, 2, 3)
    all_lse, all_delta = (
        lax.all_gather(jnp.swapaxes(log_total, 2, 3), "ctx", axis=2, tiled=True),
        lax.all_gather(row_delta, "ctx", axis=2, tiled=True),
    )
    partner_lse = jnp.swapaxes(
        lax.dynamic_slice_in_dim(all_lse, partner * unit_rows, unit_rows, 2), 2, 3
    )
    partner_delta = jnp.swapaxes(
        lax.dynamic_slice_in_dim(all_delta, partner * unit_rows, unit_rows, 2), 2, 3
    )
    far_queries, far_grads = from_partner((q_seq, grad_seq), "ctx", 0)
    near_queries = jnp.concatenate([q_heads, heads_of(far_queries, head_count)], axis=2)
    near_grads = jnp.concatenate([grad_heads, heads_of(far_grads, head_count)], axis=2)
    near_lse = jnp.concatenate([log_total, partner_lse], axis=3)
    near_delta = jnp.concatenate([delta_heads, partner_delta], axis=3)
    local_scores = (
        jnp.einsum(
            "jpqhe,jpkhe->jphqk", near_queries, near_keys, preferred_element_type=jnp.float32
        )
        * score_scale
    )
    probabilities = jnp.exp(local_scores - near_lse[..., None])
    grad_probs = jnp.einsum(
        "jpqhe,jpkhe->jphqk", near_grads, near_values, preferred_element_type=jnp.float32
    )
    grad_scores = (probabilities * (grad_probs - near_delta[..., None])).astype(jnp.bfloat16)
    grad_q_local = (
        jnp.einsum(
            "jphqk,jpkhe->jpqhe",
            grad_scores[:, :, :, :unit_rows, :],
            near_keys,
            preferred_element_type=jnp.float32,
        )
        * score_scale
    )
    grad_k_local = (
        jnp.einsum(
            "jphqk,jpqhe->jpkhe",
            grad_scores[..., :unit_rows],
            near_queries,
            preferred_element_type=jnp.float32,
        )
        * score_scale
    )
    grad_v_local = jnp.einsum(
        "jphqk,jpqhe->jpkhe",
        probabilities.astype(jnp.bfloat16)[..., :unit_rows],
        near_grads,
        preferred_element_type=jnp.float32,
    )
    query_stepper = partial(
        query_grad_step,
        q_heads,
        grad_heads,
        log_total,
        delta_heads,
        my_block,
        score_scale,
        head_count,
    )
    key_stepper = partial(key_grad_step, k_heads, v_heads, my_block, score_scale, head_count)

    def query_piece(carried, pieces, offset):
        return group_loop(pieces, unit_rows, block_pairs, query_stepper, carried)

    def key_piece(carried, pieces, offset):
        return group_loop(
            (pieces[0], pieces[1], all_lse, all_delta), unit_rows, block_pairs, key_stepper, carried
        )

    grad_q_all = query_piece(
        grad_q_local,
        (
            lax.all_gather(k_seq, "ctx", axis=2, tiled=True),
            lax.all_gather(v_seq, "ctx", axis=2, tiled=True),
        ),
        jnp.int32(0),
    )
    grad_k_all, grad_v_all = key_piece(
        (grad_k_local, grad_v_local),
        (
            lax.all_gather(q_seq, "ctx", axis=2, tiled=True),
            lax.all_gather(grad_seq, "ctx", axis=2, tiled=True),
        ),
        jnp.int32(0),
    )
    grad_queries = grad_q_all.reshape(row_count, model_width).astype(jnp.bfloat16)
    grad_keys = grad_k_all.reshape(row_count, model_width).astype(jnp.bfloat16)
    grad_values = grad_v_all.reshape(row_count, model_width).astype(jnp.bfloat16)
    grad_mixed = jnp.concatenate([grad_queries, grad_keys, grad_values], axis=1)
    grad_qkv = jnp.dot(normed.T, grad_mixed, preferred_element_type=jnp.float32)
    grad_bquery = jnp.sum(grad_queries.astype(jnp.float32), axis=0)
    grad_bvalue = jnp.sum(grad_values.astype(jnp.float32), axis=0)
    grad_normed = jnp.dot(grad_mixed, w_qkv.T, preferred_element_type=jnp.float32)
    _, norm_back_one = jax.vjp(
        layer_norm, inputs, gain_one.astype(jnp.float32), bias_one.astype(jnp.float32)
    )
    grad_inputs, grad_gain_one, grad_bias_one = norm_back_one(grad_normed)
    grad_hidden = (grad_inputs + grad_middle).astype(jnp.bfloat16)
    totals = (
        lax.psum_scatter(grad_gain_one, "ctx", scatter_dimension=0, tiled=True),
        lax.psum_scatter(grad_bias_one, "ctx", scatter_dimension=0, tiled=True),
        lax.psum_scatter(grad_qkv, "ctx", scatter_dimension=0, tiled=True),
        lax.psum_scatter(grad_bquery, "ctx", scatter_dimension=0, tiled=True),
        lax.psum_scatter(grad_bvalue, "ctx", scatter_dimension=0, tiled=True),
        lax.psum_scatter(grad_wout, "ctx", scatter_dimension=0, tiled=True),
        lax.psum_scatter(grad_bout, "ctx", scatter_dimension=0, tiled=True),
        lax.psum_scatter(grad_gain_two, "ctx", scatter_dimension=0, tiled=True),
        lax.psum_scatter(grad_bias_two, "ctx", scatter_dimension=0, tiled=True),
        lax.psum_scatter(grad_fc, "ctx", scatter_dimension=0, tiled=True),
        lax.psum_scatter(grad_bfc, "ctx", scatter_dimension=0, tiled=True),
        lax.psum_scatter(grad_proj, "ctx", scatter_dimension=0, tiled=True),
        lax.psum_scatter(grad_bproj, "ctx", scatter_dimension=0, tiled=True),
    )
    return (
        layer_out,
        grad_hidden,
        totals[0],
        totals[1],
        totals[2],
        totals[3],
        totals[4],
        totals[5],
        totals[6],
        totals[7],
        totals[8],
        totals[9],
        totals[10],
        totals[11],
        totals[12],
    )


def solution(mesh):
    return jax.shard_map(
        shards,
        mesh=mesh,
        in_specs=(
            P("ctx", None),
            P(),
            P("ctx"),
            P("ctx"),
            P("ctx", None),
            P("ctx"),
            P("ctx"),
            P("ctx", None),
            P("ctx"),
            P("ctx"),
            P("ctx"),
            P("ctx", None),
            P("ctx"),
            P("ctx", None),
            P("ctx"),
            P("ctx", None),
        ),
        out_specs=(
            P("ctx", None),
            P("ctx", None),
            P("ctx"),
            P("ctx"),
            P("ctx", None),
            P("ctx"),
            P("ctx"),
            P("ctx", None),
            P("ctx"),
            P("ctx"),
            P("ctx"),
            P("ctx", None),
            P("ctx"),
            P("ctx", None),
            P("ctx"),
        ),
        check_vma=False,
    )
```

profile of v0, /device:TPU:0, one launch (start us, length us, event | category | flops | bytes accessed | tf_op | source)
XLA Modules:
  0.0 1421.4 jit_solution(11220400322978021832)
XLA Ops:
  15.5 42.8 %all-reduce.19 = (bf16[768]{0:T(1024)(128)(2,1)S(1)}, bf16[768]{0:T(1024)(128)(2,1)S(1)}, bf16[768]{0:T(1024)(128)(2,1)S(1)}, bf16[768]{0:T(1024)(128)(2,1)S(1)}...) all-reduce(bf16[768]{0:T(1024)(128)(2,1)S(1)} %dynamic-update-slice, ...), channel_id=1, replica_groups=mesh['ctx'=32] {'ctx'}, use_global_device_ids=true, to_apply=%add.1 | all-reduce | flops 9216 | bytes 36864
  61.7 12.0 all-gather.9.cloned.1.call-done
  112.4 122.6 %all-gather.11.cloned.1.call-done = bf16[2,2,4096,768]{3,2,1,0:T(8,128)(2,1)} async-done(((bf16[2,2,128,768]{3,2,1,0:T(8,128)(2,1)}), bf16[2,2,4096,768]{3,2,1,0:T(8,128)(2,1)}) %all-gather.11.cloned.1.call-update) | async-done | bytes 25165840 | tf_op jit(solution)/shard_map/all_gather | solution.py:307
  235.0 32.7 %copy.204 = bf16[2,2,32,128,768]{3,4,2,0,1:T(8,128)(2,1)} copy(bf16[2,2,32,128,768]{4,3,2,1,0:T(8,128)(2,1)} %bitcast.331) | data formatting | bytes 50331648 | tf_op jit(solution)/shard_map/while | solution.py:86
  267.6 123.0 %all-gather.13.cloned.1.call-done = bf16[2,2,4096,768]{3,2,1,0:T(8,128)(2,1)} async-done(((bf16[2,2,128,768]{3,2,1,0:T(8,128)(2,1)}), bf16[2,2,4096,768]{3,2,1,0:T(8,128)(2,1)}) %all-gather.13.cloned.1.call-update) | async-done | bytes 25165840 | tf_op jit(solution)/shard_map/all_gather | solution.py:308
  390.7 32.6 %copy.205 = bf16[2,2,32,128,768]{3,4,2,0,1:T(8,128)(2,1)} copy(bf16[2,2,32,128,768]{4,3,2,1,0:T(8,128)(2,1)} %bitcast.332) | data formatting | bytes 50331648 | tf_op jit(solution)/shard_map/while | solution.py:86
  423.3 138.3 %while.45 = (s32[]{:T(128)}, f32[2,2,12,128]{3,2,1,0:T(8,128)S(1)}, f32[2,2,12,128]{3,2,1,0:T(8,128)S(1)}, f32[2,2,128,12,64]{2,4,3,1,0:T(8,128)}, s32[32]{0:T(1...) while((s32[]{:T(128)}, f32[2,2,12,128]{3,2,1,0:T(8,128)S(1)}, ...), condition=%wide.region_11.12_spmd, body=%wide.region_5.11_spmd.sunk | while | flops 857794624 | bytes 110815160 | solution.py:86
  424.2 10.8 constant_dynamic-slice_fusion.15
  458.6 10.6 constant_dynamic-slice_fusion.15
  492.9 10.8 constant_dynamic-slice_fusion.15
  527.4 10.7 constant_dynamic-slice_fusion.15
  581.6 9.8 convert_reduce_fusion
  625.0 47.5 %all_gather.74 = f32[2,2,4096,12]{2,3,0,1:T(8,128)} all-gather(f32[2,2,128,12]{2,3,0,1:T(8,128)S(1)} %bitcast.347), channel_id=1, replica_groups=mesh['ctx'=32] {'ctx'}, dimensions={2}, use_global_device_ids=true | all-gather | bytes 811008 | tf_op jit(solution)/shard_map/all_gather | solution.py:358
  672.4 42.7 %all_gather.75 = f32[2,2,4096,12]{2,1,0,3:T(2,128)S(1)} all-gather(f32[2,2,128,12]{2,1,0,3:T(2,128)S(1)} %multiply_reduce_fusion.2), channel_id=1, replica_groups=mesh['ctx'=32] {'ctx'}, dimensions={2}, use_global_device_ids=true | all-gather | bytes 811008 | tf_op jit(solution)/shard_map/all_gather | solution.py:359
  715.1 10.7 fusion.169
  733.2 9.9 subtract_exponential_fusion.1
  758.4 177.6 %while.46 = (s32[]{:T(128)}, f32[2,2,128,12,64]{2,4,3,1,0:T(8,128)}, s32[32]{0:T(128)S(1)}, s32[]{:T(128)}, bf16[2,2,32,128,768]{3,4,2,0,1:T(8,128)(2,1)}, /*ind...) while((s32[]{:T(128)}, ...), condition=%wide.region_19.20_spmd, body=%wide.region_17.19_spmd.sunk | while | flops 1242611712 | bytes 105991552 | solution.py:86
  759.7 10.7 constant_dynamic-slice_fusion.16
  770.3 9.4 fusion.229
  779.9 17.2 %multiply_bitcast_fusion.6 = f32[2,8,128,12,64]{2,4,3,1,0:T(8,128)} fusion(f32[2,8,12,128,128]{4,3,2,1,0:T(8,128)} %fusion.229, f32[2,8,12,128]{3,2,1,0:T(8,128)S(1)} %get-tuple-element.1077, f32[2,8,12,128]{3,2,1,0:T(8,128)S(1)} %get-tuple-element.1078, pred[8]{0:T(512)(128)(4,1)S(1)} %get-tuple-element.1079, ...), kind=kOutput, calls=%fused_computation.49.clone.1 | convolution fusion | flops 830472192 | bytes 32507904 | tf_op jit(solution)/shard_map/while/body/eval_jaxpr/jghqk,jgkhe->jgqhe/dot_general | solution.py:156
  803.8 10.6 constant_dynamic-slice_fusion.16
  814.4 9.4 fusion.229
  823.9 18.7 %multiply_bitcast_fusion.6 = f32[2,8,128,12,64]{2,4,3,1,0:T(8,128)} fusion(f32[2,8,12,128,128]{4,3,2,1,0:T(8,128)} %fusion.229, f32[2,8,12,128]{3,2,1,0:T(8,128)S(1)} %get-tuple-element.1077, f32[2,8,12,128]{3,2,1,0:T(8,128)S(1)} %get-tuple-element.1078, pred[8]{0:T(512)(128)(4,1)S(1)} %get-tuple-element.1079, ...), kind=kOutput, calls=%fused_computation.49.clone.1 | convolution fusion | flops 830472192 | bytes 32507904 | tf_op jit(solution)/shard_map/while/body/eval_jaxpr/jghqk,jgkhe->jgqhe/dot_general | solution.py:156
  849.2 10.8 constant_dynamic-slice_fusion.16
  860.0 9.4 fusion.229
  869.4 16.5 %multiply_bitcast_fusion.6 = f32[2,8,128,12,64]{2,4,3,1,0:T(8,128)} fusion(f32[2,8,12,128,128]{4,3,2,1,0:T(8,128)} %fusion.229, f32[2,8,12,128]{3,2,1,0:T(8,128)S(1)} %get-tuple-element.1077, f32[2,8,12,128]{3,2,1,0:T(8,128)S(1)} %get-tuple-element.1078, pred[8]{0:T(512)(128)(4,1)S(1)} %get-tuple-element.1079, ...), kind=kOutput, calls=%fused_computation.49.clone.1 | convolution fusion | flops 830472192 | bytes 32507904 | tf_op jit(solution)/shard_map/while/body/eval_jaxpr/jghqk,jgkhe->jgqhe/dot_general | solution.py:156
  892.7 11.2 constant_dynamic-slice_fusion.16
  903.9 9.4 fusion.229
  913.4 16.7 %multiply_bitcast_fusion.6 = f32[2,8,128,12,64]{2,4,3,1,0:T(8,128)} fusion(f32[2,8,12,128,128]{4,3,2,1,0:T(8,128)} %fusion.229, f32[2,8,12,128]{3,2,1,0:T(8,128)S(1)} %get-tuple-element.1077, f32[2,8,12,128]{3,2,1,0:T(8,128)S(1)} %get-tuple-element.1078, pred[8]{0:T(512)(128)(4,1)S(1)} %get-tuple-element.1079, ...), kind=kOutput, calls=%fused_computation.49.clone.1 | convolution fusion | flops 830472192 | bytes 32507904 | tf_op jit(solution)/shard_map/while/body/eval_jaxpr/jghqk,jgkhe->jgqhe/dot_general | solution.py:156
  945.3 320.7 %while.47 = (s32[]{:T(128)}, f32[2,2,128,12,64]{2,4,3,1,0:T(8,128)S(1)}, f32[2,2,128,12,64]{2,4,3,1,0:T(8,128)S(1)}, s32[]{:T(128)}, s32[32]{0:T(128)S(1)}, /*in...) while((s32[]{:T(128)}, ...), condition=%wide.region_23.24_spmd, body=%wide.region_20.23_spmd.sunk | while | flops 1665712128 | bytes 158961136 | solution.py:86
  949.1 10.7 constant_dynamic-slice_fusion.17
  968.5 9.5 fusion.237
  989.4 11.5 fusion.239
  1000.9 16.5 %multiply_bitcast_fusion.7 = f32[2,8,128,12,64]{2,4,3,1,0:T(8,128)} fusion(f32[2,8,12,128,128]{4,3,2,1,0:T(8,128)} %fusion.237, f32[2,8,12,128]{3,2,1,0:T(8,128)} %get-tuple-element.1107, f32[2,8,12,128]{3,2,1,0:T(8,128)} %get-tuple-element.1103, pred[8]{0:T(512)(128)(4,1)S(1)} %get-tuple-element.1104, pred[8]{0:T(512)(128)(4,1)S(1)} %get-tuple-element.1095, ...), kind=kOutput, calls=%fused_computation.97.clone.1 | convolution fusion | flops 830472192 | bytes 32442368 | tf_op jit(solution)/shard_map/while/body/eval_jaxpr/jghqk,jgqhe->jgkhe/dot_general | solution.py:185
  1028.6 11.4 constant_dynamic-slice_fusion.17
  1048.8 9.8 fusion.237
  1069.9 11.5 fusion.239
  1081.5 16.6 %multiply_bitcast_fusion.7 = f32[2,8,128,12,64]{2,4,3,1,0:T(8,128)} fusion(f32[2,8,12,128,128]{4,3,2,1,0:T(8,128)} %fusion.237, f32[2,8,12,128]{3,2,1,0:T(8,128)} %get-tuple-element.1107, f32[2,8,12,128]{3,2,1,0:T(8,128)} %get-tuple-element.1103, pred[8]{0:T(512)(128)(4,1)S(1)} %get-tuple-element.1104, pred[8]{0:T(512)(128)(4,1)S(1)} %get-tuple-element.1095, ...), kind=kOutput, calls=%fused_computation.97.clone.1 | convolution fusion | flops 830472192 | bytes 32442368 | tf_op jit(solution)/shard_map/while/body/eval_jaxpr/jghqk,jgqhe->jgkhe/dot_general | solution.py:185
  1109.0 10.9 constant_dynamic-slice_fusion.17
  1128.6 9.5 fusion.237
  1149.6 11.4 fusion.239
  1161.0 17.1 %multiply_bitcast_fusion.7 = f32[2,8,128,12,64]{2,4,3,1,0:T(8,128)} fusion(f32[2,8,12,128,128]{4,3,2,1,0:T(8,128)} %fusion.237, f32[2,8,12,128]{3,2,1,0:T(8,128)} %get-tuple-element.1107, f32[2,8,12,128]{3,2,1,0:T(8,128)} %get-tuple-element.1103, pred[8]{0:T(512)(128)(4,1)S(1)} %get-tuple-element.1104, pred[8]{0:T(512)(128)(4,1)S(1)} %get-tuple-element.1095, ...), kind=kOutput, calls=%fused_computation.97.clone.1 | convolution fusion | flops 830472192 | bytes 32442368 | tf_op jit(solution)/shard_map/while/body/eval_jaxpr/jghqk,jgqhe->jgkhe/dot_general | solution.py:185
  1189.4 11.3 constant_dynamic-slice_fusion.17
  1209.3 9.5 fusion.237
  1230.2 11.7 fusion.239
  1241.9 16.5 %multiply_bitcast_fusion.7 = f32[2,8,128,12,64]{2,4,3,1,0:T(8,128)} fusion(f32[2,8,12,128,128]{4,3,2,1,0:T(8,128)} %fusion.237, f32[2,8,12,128]{3,2,1,0:T(8,128)} %get-tuple-element.1107, f32[2,8,12,128]{3,2,1,0:T(8,128)} %get-tuple-element.1103, pred[8]{0:T(512)(128)(4,1)S(1)} %get-tuple-element.1104, pred[8]{0:T(512)(128)(4,1)S(1)} %get-tuple-element.1095, ...), kind=kOutput, calls=%fused_computation.97.clone.1 | convolution fusion | flops 830472192 | bytes 32442368 | tf_op jit(solution)/shard_map/while/body/eval_jaxpr/jghqk,jgqhe->jgkhe/dot_general | solution.py:185
  1296.2 45.6 %all-reduce.18 = (f32[768]{0:T(1024)S(1)}, f32[768]{0:T(1024)S(1)}, f32[768]{0:T(1024)S(1)}, f32[768]{0:T(1024)S(1)}, f32[768]{0:T(1024)S(1)}, /*index=5*/f32[76...) all-reduce(f32[768]{0:T(1024)S(1)} %get-tuple-element.685, ...), channel_id=2, replica_groups=mesh['ctx'=32] {'ctx'}, use_global_device_ids=true, to_apply=%region_27.28.clone | all-reduce | flops 9216 | bytes 73728
  1347.0 67.3 %reduce-scatter.5.cloned.1.call-done = f32[24,2304]{1,0:T(8,128)} async-done(((f32[768,2304]{1,0:T(8,128)}), f32[24,2304]{1,0:T(8,128)}) %reduce-scatter.5.cloned.1.call-update) | async-done | bytes 221200 | tf_op jit(solution)/shard_map/reduce_scatter | solution.py:459
  (484 shorter events, 416.9 us)
Async XLA Ops:
  7.2 66.6 %all-gather.9.cloned.1.call-start = ((), (), s32[]{:S(2)}) async-start(), calls=%async_computation.4 | async-start | bytes 3649536 | tf_op jit(solution)/shard_map/all_gather | solution.py:233
  7.9 227.0 %all-gather.11.cloned.1.call-start = ((), (), s32[]{:S(2)}) async-start(), calls=%async_computation.5 | async-start | bytes 25952256 | tf_op jit(solution)/shard_map/all_gather | solution.py:307
  58.3 19.9 %copy-start.54 = (f32[768]{0:T(1024)}, f32[768]{0:T(1024)S(1)}, u32[]{:S(2)}) copy-start(f32[768]{0:T(1024)S(1)} %convert_element_type.148) | copy-start | bytes 9220
  58.3 19.9 %copy-start.37 = (f32[768]{0:T(1024)}, f32[768]{0:T(1024)S(1)}, u32[]{:S(2)}) copy-start(f32[768]{0:T(1024)S(1)} %convert_element_type.147) | copy-start | bytes 9220
  59.6 18.6 %copy-start.39 = (f32[512]{0:T(512)}, f32[512]{0:T(512)S(1)}, u32[]{:S(2)}) copy-start(f32[512]{0:T(512)S(1)} %broadcast_multiply_fusion.1) | copy-start | bytes 6148
  61.7 16.5 %copy-start.42 = (f32[512]{0:T(512)}, f32[512]{0:T(512)S(1)}, u32[]{:S(2)}) copy-start(f32[512]{0:T(512)S(1)} %fusion.151) | copy-start | bytes 6148
  81.3 309.3 %all-gather.13.cloned.1.call-start = ((), (), s32[]{:S(2)}) async-start(), calls=%async_computation.6 | async-start | bytes 25952256 | tf_op jit(solution)/shard_map/all_gather | solution.py:308
  81.4 9.0 copy-start.63
  84.7 8.8 copy-start.18
  84.7 9.1 copy-start.22
  84.8 484.3 %all-gather.15.cloned.1.call-start = ((), (), s32[]{:S(2)}) async-start(), calls=%async_computation.7 | async-start | bytes 1216512 | tf_op jit(solution)/shard_map/all_gather | solution.py:236
  85.3 487.8 %all-gather.17.cloned.1.call-start = ((), (), s32[]{:S(2)}) async-start(), calls=%async_computation.8 | async-start | bytes 4866048 | tf_op jit(solution)/shard_map/all_gather | solution.py:240
  85.9 495.6 %all-gather.19.cloned.1.call-start = ((), (), s32[]{:S(2)}) async-start(), calls=%async_computation.9 | async-start | bytes 4866048 | tf_op jit(solution)/shard_map/all_gather | solution.py:242
  86.5 858.8 %all-gather.21.cloned.1.call-start = ((), (), s32[]{:S(2)}) async-start(), calls=%async_computation.10 | async-start | bytes 25952256 | tf_op jit(solution)/shard_map/all_gather | solution.py:438
  87.3 858.0 %all-gather.23.cloned.1.call-start = ((), (), s32[]{:S(2)}) async-start(), calls=%async_computation.11 | async-start | bytes 25952256 | tf_op jit(solution)/shard_map/all_gather | solution.py:439
  87.5 12.6 collective-permute-start
  87.8 14.7 %collective-permute-start.1 = (bf16[2,2,128,768]{3,2,1,0:T(8,128)(2,1)}, bf16[2,2,128,768]{3,2,1,0:T(8,128)(2,1)}, u32[]{:S(2)}, u32[]{:S(2)}) collective-permute-start(bf16[2,2,128,768]{3,2,1,0:T(8,128)(2,1)} %bitcast.340), channel_id=1, source_target_pairs={{0,1},{1,0},{2,3},{3,2},{4,5},{5,4},{6,7},{7,6},{8,9},{9,8},{10,11... | collective-permute-start | bytes 2359304 | tf_op jit(solution)/shard_map/ppermute | solution.py:17
  98.5 6.2 copy-start.10
  99.9 9.6 copy-start.13
  561.6 7.5 copy-start.8
  561.6 7.5 copy-start.57
  573.1 8.5 copy-start.30
  573.1 8.5 copy-start.51
  581.6 9.8 copy-start.26
  581.6 9.8 copy-start.61
  599.1 747.9 %reduce-scatter.7.cloned.1.call-start = ((), (), s32[]{:S(2)}) async-start(), calls=%async_computation.13 | async-start | bytes 2433024 | tf_op jit(solution)/shard_map/reduce_scatter | solution.py:462
  602.5 744.5 %reduce-scatter.9.cloned.1.call-start = ((), (), s32[]{:S(2)}) async-start(), calls=%async_computation.14 | async-start | bytes 9732096 | tf_op jit(solution)/shard_map/reduce_scatter | solution.py:466
  611.5 735.5 %reduce-scatter.11.cloned.1.call-start = ((), (), s32[]{:S(2)}) async-start(), calls=%async_computation.15 | async-start | bytes 9732096 | tf_op jit(solution)/shard_map/reduce_scatter | solution.py:468
  612.6 5.9 collective-permute-start.2
  622.3 120.8 %collective-permute-start.3 = (bf16[2,2,128,768]{3,2,1,0:T(8,128)(2,1)}, bf16[2,2,128,768]{3,2,1,0:T(8,128)(2,1)}, u32[]{:S(2)}, u32[]{:S(2)}) collective-permute-start(bf16[2,2,128,768]{3,2,1,0:T(8,128)(2,1)} %bitcast.64), channel_id=1, source_target_pairs={{0,1},{1,0},{2,3},{3,2},{4,5},{5,4},{6,7},{7,6},{8,9},{9,8},{10,11... | collective-permute-start | bytes 2359304 | tf_op jit(solution)/shard_map/ppermute | solution.py:17
  715.1 10.7 copy-start.29
  732.2 682.2 %reduce-scatter.5.cloned.1.call-start = ((), (), s32[]{:S(2)}) async-start(), calls=%async_computation.12 | async-start | bytes 7299072 | tf_op jit(solution)/shard_map/reduce_scatter | solution.py:459
  733.2 12.2 copy-start.14
  745.4 6.9 copy-start.23
  745.4 6.9 copy-start.24
  745.4 11.1 slice-start
  745.4 11.1 slice-start.1
  935.9 9.3 copy-start
  935.9 9.3 copy-start.3
  989.4 11.5 copy-start.50
  989.4 11.5 copy-start.12
  1069.9 11.6 copy-start.50
  1069.9 11.6 copy-start.12
  1149.6 11.4 copy-start.50
  1149.6 11.5 copy-start.12
  1230.2 11.7 copy-start.50
  1230.2 11.7 copy-start.12
  1278.9 9.1 copy-start.41
  (54 other events, 142.0 us)
Sparse Core Ops, SparseCore 0:
  10.9 62.8 all-gather.8
  81.5 153.4 all-gather.10
  237.8 152.8 all-gather.12
  393.4 52.3 all-gather.14
  448.5 62.4 all-gather.16
  513.7 62.4 all-gather.18
  579.1 167.5 all-gather.20
  749.6 153.1 all-gather.22
  908.7 97.2 reduce-scatter.6
  1013.3 134.5 reduce-scatter.8
  1154.3 134.6 reduce-scatter.10
  1296.1 118.1 reduce-scatter.4
where the time goes:
time: 1430 us; the launch traced here: 1420 us
  matrix products  412 us (29%)
  local copies, waits for them, and re-layouts  362 us (25%)
  waiting for transfers between devices  328 us (23%)
  blocking collectives  178 us (12%)
  other arithmetic  122 us (9%)
  between operations  15.3 us (1%)
    dynamic_slice x20, local copies, waits for them, and re-layouts, one_turn(): lax.dynamic_slice_in_dim(item, position * batch_groups, batch_groups, 2)  200 us
    all_gather x1, waiting for transfers between devices, shards(): lax.all_gather(v_seq, 'ctx', axis=2, tiled=True)  123 us
    all_gather x1, waiting for transfers between devices, shards(): lax.all_gather(k_seq, 'ctx', axis=2, tiled=True)  123 us
    unnamed x2, blocking collectives  88.3 us
    while x7, local copies, waits for them, and re-layouts, group_loop(): return lax.fori_loop(0, turn_count, one_turn, carried)  70.1 us
    dot_general x4, matrix products, query_grad_step(): jnp.einsum('jghqk,jgkhe->jgqhe', grad_scores, key_sel, preferred_element_...  69.1 us
    reduce_scatter x1, waiting for transfers between devices, shards(): lax.psum_scatter(grad_qkv, 'ctx', scatter_dimension=0, tiled=True)  67.3 us
    dot_general x4, matrix products, key_grad_step(): jnp.einsum('jghqk,jgqhe->jgkhe', grad_scores, query_sel, preferred_elemen...  66.7 us
  transfers between devices with their start and end apart: 16, of which 4 were waited for; matrix products, arithmetic and copies ran while one was open for 61% of the time, Pallas kernels for 0%

commit v1 on v0

--- a/solution.py
+++ b/solution.py
@@ -5,6 +5,9 @@
 import jax.numpy as jnp
 from jax import lax
 from jax.sharding import PartitionSpec as P
+from jax.experimental import pallas as pl
+from jax.experimental.pallas import tpu as pltpu
+from jax.sharding import Mesh
 
 HEADS = 12
 SEQS = 4
@@ -487,7 +490,184 @@
     )
 
 
-def solution(mesh):
+HD = 64
+
+
+def attend_kernel(inv, q_ref, k_ref, v_ref, o_ref, lse_ref, qt, ks, vt):
+    W = q_ref.shape[1]
+    nh = W // HD
+    npair = inv.shape[0]
+    U = q_ref.shape[0] // npair
+    B = k_ref.shape[0] // npair
+    TQ, TK = 2 * U, 2 * B
+
+    @pl.loop(0, npair)
+    def _(i):
+        p = inv[i]
+        qc = q_ref[pl.ds(p * U, U), :]
+        qt[:, pl.ds(pl.multiple_of(i * U, U), U)] = qc.T
+        kc = k_ref[pl.ds(p * B, B), :]
+        for h in range(nh):
+            ks[h, pl.ds(i * B, B), :] = kc[:, h * HD:(h + 1) * HD]
+        vc = v_ref[pl.ds(p * B, B), :]
+        vct = vc.T
+        for h in range(nh):
+            vt[h, 0:HD, pl.ds(pl.multiple_of(i * B, B), B)] = vct[h * HD:(h + 1) * HD]
+            vt[h, HD:, pl.ds(pl.multiple_of(i * B, B), B)] = jnp.ones((vt.shape[1] - HD, B), vt.dtype)
+
+    def tile(m, c, carry, masked):
+        out = []
+        for h in range(nh):
+            mx, acc = carry[h]
+            qh = qt[h * HD:(h + 1) * HD, pl.ds(pl.multiple_of(m * TQ, TQ), TQ)]
+            kh = ks[h, pl.ds(pl.multiple_of(c * TK, TK), TK), :]
+            s = jnp.dot(kh, qh, preferred_element_type=jnp.float32)
+            if masked:
+                row = lax.broadcasted_iota(jnp.int32, s.shape, 0)
+                col = lax.broadcasted_iota(jnp.int32, s.shape, 1)
+                s = jnp.where((row >= B) & (col < U), NEG, s)
+            new = jnp.maximum(mx, jnp.max(s, axis=0, keepdims=True))
+            p = jnp.exp(s - new).astype(jnp.bfloat16)
+            vh = vt[h, :, pl.ds(pl.multiple_of(c * TK, TK), TK)]
+            acc = acc * jnp.exp(mx - new) + jnp.dot(vh, p, preferred_element_type=jnp.float32)
+            out.append((new, acc))
+        return tuple(out)
+
+    @pl.loop(0, npair // 2)
+    def _(m):
+        init = tuple((jnp.full((1, TQ), NEG, jnp.float32), jnp.zeros((vt.shape[1], TQ), jnp.float32)) for _ in range(nh))
+        carry = lax.fori_loop(0, m, lambda c, x: tile(m, c, x, False), init)
+        carry = tile(m, m, carry, True)
+        outs = []
+        for h in range(nh):
+            mx, acc = carry[h]
+            tot = acc[HD:HD + 1]
+            outs.append(acc[:HD] / tot)
+            lse_ref[h:h + 1, pl.ds(pl.multiple_of(m * TQ, TQ), TQ)] = mx + jnp.log(tot)
+        o = jnp.concatenate(outs, axis=0).T
+        for half in range(2):
+            o_ref[pl.ds(inv[2 * m + half] * U, U), :] = o[half * U:(half + 1) * U]
+
+
+def attend(inv, q, k, v):
+    R, W = q.shape
+    K = k.shape[0]
+    nh = W // HD
+    return pl.pallas_call(
+        attend_kernel,
+        grid_spec=pltpu.PrefetchScalarGridSpec(
+            num_scalar_prefetch=1, grid=(),
+            in_specs=[pl.BlockSpec(memory_space=pltpu.VMEM)] * 3,
+            out_specs=[pl.BlockSpec(memory_space=pltpu.VMEM)] * 2,
+            scratch_shapes=[
+                pltpu.VMEM((W, R), jnp.bfloat16),
+                pltpu.VMEM((nh, K, HD), jnp.bfloat16),
+                pltpu.VMEM((nh, HD + 16, K), jnp.bfloat16),
+            ]),
+        out_shape=[jax.ShapeDtypeStruct((R, W), jnp.float32), jax.ShapeDtypeStruct((8, R), jnp.float32)],
+        compiler_params=pltpu.CompilerParams(vmem_limit_bytes=56 << 20),
+        name="attend",
+    )(inv, q, k, v)
+
+
+def attend_back_kernel(inv, q_ref, k_ref, v_ref, g_ref, o_ref, lse_ref, dq_ref, dk_ref, dv_ref,
+                       qt, gt, qx, gx, ks, vs, kt, delta, dkv):
+    W = q_ref.shape[1]
+    nh = W // HD
+    npair = inv.shape[0]
+    U = q_ref.shape[0] // npair
+    B = k_ref.shape[0] // npair
+    TQ, TK = 2 * U, 2 * B
+
+    @pl.loop(0, npair)
+    def _(i):
+        p = inv[i]
+        qc = q_ref[pl.ds(p * U, U), :]
+        gc = g_ref[pl.ds(p * U, U), :]
+        oc = o_ref[pl.ds(p * U, U), :]
+        cols = pl.ds(pl.multiple_of(i * U, U), U)
+        qt[:, cols] = qc.T
+        gt[:, cols] = gc.T
+        prod = (oc * gc.astype(jnp.float32)).T
+        zero = jnp.zeros((U, HD), jnp.bfloat16)
+        for h in range(nh):
+            delta[h:h + 1, cols] = jnp.sum(prod[h * HD:(h + 1) * HD], axis=0, keepdims=True)
+            qx[h, pl.ds(i * U, U), :] = jnp.concatenate([zero, qc[:, h * HD:(h + 1) * HD]], axis=1)
+            gx[h, pl.ds(i * U, U), :] = jnp.concatenate([gc[:, h * HD:(h + 1) * HD], zero], axis=1)
+        kc = k_ref[pl.ds(p * B, B), :]
+        vc = v_ref[pl.ds(p * B, B), :]
+        kt[:, pl.ds(pl.multiple_of(i * B, B), B)] = kc.T
+        for h in range(nh):
+            ks[h, pl.ds(i * B, B), :] = kc[:, h * HD:(h + 1) * HD]
+            vs[h, pl.ds(i * B, B), :] = vc[:, h * HD:(h + 1) * HD]
+    dkv[...] = jnp.zeros_like(dkv)
+
+    def tile(m, c, carry, masked):
+        out = []
+        qcols = pl.ds(pl.multiple_of(m * TQ, TQ), TQ)
+        krows = pl.ds(pl.multiple_of(c * TK, TK), TK)
+        for h in range(nh):
+            hs = slice(h * HD, (h + 1) * HD)
+            s = jnp.dot(ks[h, krows, :], qt[hs, qcols], preferred_element_type=jnp.float32)
+            p = jnp.exp(s - lse_ref[h:h + 1, qcols])
+            if masked:
+                row = lax.broadcasted_iota(jnp.int32, s.shape, 0)
+                col = lax.broadcasted_iota(jnp.int32, s.shape, 1)
+                p = jnp.where((row >= B) & (col < U), 0.0, p)
+            dp = jnp.dot(vs[h, krows, :], gt[hs, qcols], preferred_element_type=jnp.float32)
+            ds = (p * (dp - delta[h:h + 1, qcols])).astype(jnp.bfloat16)
+            pl_ = p.astype(jnp.bfloat16)
+            dkv[h, krows, :] += (jnp.dot(pl_, gx[h, qcols, :], preferred_element_type=jnp.float32)
+                                 + jnp.dot(ds, qx[h, qcols, :], preferred_element_type=jnp.float32))
+            out.append(carry[h] + jnp.dot(kt[hs, krows], ds, preferred_element_type=jnp.float32))
+        return tuple(out)
+
+    @pl.loop(0, npair // 2)
+    def _(m):
+        init = tuple(jnp.zeros((HD, TQ), jnp.float32) for _ in range(nh))
+        carry = lax.fori_loop(0, m, lambda c, x: tile(m, c, x, False), init)
+        carry = tile(m, m, carry, True)
+        dq = jnp.concatenate(carry, axis=0).T * 0.125
+        for half in range(2):
+            dq_ref[pl.ds(inv[2 * m + half] * U, U), :] = dq[half * U:(half + 1) * U].astype(dq_ref.dtype)
+
+    @pl.loop(0, npair)
+    def _(i):
+        rows = pl.ds(inv[i] * B, B)
+        parts = [dkv[h, pl.ds(i * B, B), :] for h in range(nh)]
+        dv_ref[rows, :] = jnp.concatenate([x[:, :HD] for x in parts], axis=1)
+        dk_ref[rows, :] = jnp.concatenate([x[:, HD:] for x in parts], axis=1)
+
+
+def attend_back(inv, q, k, v, g, o, lse):
+    R, W = q.shape
+    K = k.shape[0]
+    nh = W // HD
+    return pl.pallas_call(
+        attend_back_kernel,
+        grid_spec=pltpu.PrefetchScalarGridSpec(
+            num_scalar_prefetch=1, grid=(),
+            in_specs=[pl.BlockSpec(memory_space=pltpu.VMEM)] * 6,
+            out_specs=[pl.BlockSpec(memory_space=pltpu.VMEM)] * 3,
+            scratch_shapes=[
+                pltpu.VMEM((W, R), jnp.bfloat16),
+                pltpu.VMEM((W, R), jnp.bfloat16),
+                pltpu.VMEM((nh, R, 2 * HD), jnp.bfloat16),
+                pltpu.VMEM((nh, R, 2 * HD), jnp.bfloat16),
+                pltpu.VMEM((nh, K, HD), jnp.bfloat16),
+                pltpu.VMEM((nh, K, HD), jnp.bfloat16),
+                pltpu.VMEM((W, K), jnp.bfloat16),
+                pltpu.VMEM((8, R), jnp.float32),
+                pltpu.VMEM((nh, K, 2 * HD), jnp.float32),
+            ]),
+        out_shape=[jax.ShapeDtypeStruct((R, W), jnp.bfloat16),
+                   jax.ShapeDtypeStruct((K, W), jnp.float32), jax.ShapeDtypeStruct((K, W), jnp.float32)],
+        compiler_params=pltpu.CompilerParams(vmem_limit_bytes=56 << 20),
+        name="attend_back",
+    )(inv, q, k, v, g, o, lse)
+
+
+def solution_any(mesh):
     return jax.shard_map(
         shards,
         mesh=mesh,
@@ -528,3 +708,159 @@
         ),
         check_vma=False,
     )
+
+
+AXES = ("s", "h", "r")
+PLANES = 4
+
+
+def planes(
+    hidden_in,
+    block_pairs,
+    ln1_gain,
+    ln1_bias,
+    qkv_weight,
+    query_bias,
+    value_bias,
+    out_weight,
+    out_bias,
+    ln2_gain,
+    ln2_bias,
+    fc_weight,
+    fc_bias,
+    proj_weight,
+    proj_bias,
+    out_grad,
+):
+    f32, bf16 = jnp.float32, jnp.bfloat16
+    s, h, r = (lax.axis_index(a) for a in AXES)
+    S, H, Q = (lax.axis_size(a) for a in AXES)
+    rows, D = hidden_in.shape
+    U = rows // SEQS
+    W = D // H
+    gather = lambda x: lax.all_gather(x, AXES, axis=0, tiled=True)
+    vectors = [ln1_gain, ln1_bias, query_bias, value_bias, out_bias, ln2_gain, ln2_bias, proj_bias, fc_bias]
+    sizes = [v.shape[0] for v in vectors]
+    allv = gather(jnp.concatenate(vectors)[None])
+    offs = [sum(sizes[:i]) for i in range(len(sizes))]
+    g1, b1, bq, bv, bo, g2, b2, bp, bf = (
+        allv[:, o : o + n].reshape(-1).astype(f32) for o, n in zip(offs, sizes)
+    )
+    w_out, w_fc, w_proj = gather(out_weight), gather(fc_weight), gather(proj_weight)
+    d = qkv_weight.shape[0]
+    w4 = qkv_weight.reshape(d, 3, H, W).transpose(2, 0, 1, 3).reshape(H, d, 3 * W)
+    w4 = lax.all_to_all(w4, "h", 0, 0)
+    w4 = lax.all_gather(lax.all_gather(w4, "r", axis=1), "s", axis=0)
+    w_h = w4.reshape(D, 3 * W)
+
+    blk = block_pairs[::2]
+    blk = jnp.where(s % 2 == 0, blk, blk.shape[0] - 1 - blk)
+    npair = blk.shape[0]
+    inv = jnp.sum(
+        jnp.where(blk[None, :] == jnp.arange(npair)[:, None], jnp.arange(npair)[None, :], 0), axis=1
+    ).astype(jnp.int32)
+
+    x_own = lax.all_to_all(hidden_in.reshape(S, U, D), "s", 0, 0)
+    x_all = lax.all_gather(x_own, "h", axis=1).reshape(-1, D)
+    g_own = lax.all_to_all(out_grad.reshape(S, U, D), "s", 0, 0).reshape(rows, D)
+    x_own = x_own.reshape(rows, D).astype(f32)
+
+    normed = layer_norm(x_all.astype(f32), g1, b1).astype(bf16)
+    mixed = jnp.dot(normed, w_h, preferred_element_type=f32)
+    bq_h = lax.dynamic_slice_in_dim(bq, h * W, W)
+    bv_h = lax.dynamic_slice_in_dim(bv, h * W, W)
+    q = (mixed[:, :W] + bq_h).astype(bf16)
+    k = mixed[:, W : 2 * W].astype(bf16)
+    v = (mixed[:, 2 * W :] + bv_h).astype(bf16)
+    q_scaled = q * jnp.asarray(0.125, bf16)
+
+    def from_other(t):
+        return lax.ppermute(t, "r", [(0, 1), (1, 0)])
+
+    def both(t):
+        return jnp.concatenate(
+            [t.reshape(npair, U, W), from_other(t).reshape(npair, U, W)], axis=1
+        ).reshape(npair * 2 * U, W)
+
+    k_all, v_all = both(k), both(v)
+    att, lse = attend(inv, q_scaled, k_all, v_all)
+    att_low = lax.all_to_all(att.astype(bf16).reshape(S, H, U, W), "h", 1, 1)
+    att_low = att_low.transpose(0, 2, 1, 3).reshape(rows, D)
+
+    middle = x_own + jnp.dot(att_low, w_out, preferred_element_type=f32) + bo
+    normed_two = layer_norm(middle, g2, b2).astype(bf16)
+    pre_act = jnp.dot(normed_two, w_fc, preferred_element_type=f32) + bf
+    activation = gelu_tanh(pre_act).astype(bf16)
+    layer_out = (middle + jnp.dot(activation, w_proj, preferred_element_type=f32) + bp).astype(bf16)
+    grad_out = g_own.astype(f32)
+    grad_proj = jnp.dot(activation.T, g_own, preferred_element_type=f32)
+    grad_bproj = jnp.sum(grad_out, axis=0)
+    grad_activ = jnp.dot(g_own, w_proj.T, preferred_element_type=f32)
+    _, gelu_back = jax.vjp(gelu_tanh, pre_act)
+    grad_pre = gelu_back(grad_activ)[0].astype(bf16)
+    grad_fc = jnp.dot(normed_two.T, grad_pre, preferred_element_type=f32)
+    grad_bfc = jnp.sum(grad_pre.astype(f32), axis=0)
+    grad_normed_two = jnp.dot(grad_pre, w_fc.T, preferred_element_type=f32)
+    _, norm_back_two = jax.vjp(layer_norm, middle, g2, b2)
+    grad_middle, grad_g2, grad_b2 = norm_back_two(grad_normed_two)
+    grad_middle = grad_middle + grad_out
+    grad_branch = grad_middle.astype(bf16)
+    grad_wout = jnp.dot(att_low.T, grad_branch, preferred_element_type=f32)
+    grad_bout = jnp.sum(grad_branch.astype(f32), axis=0)
+    grad_att = jnp.dot(grad_branch, w_out.T, preferred_element_type=f32).astype(bf16)
+
+    g_att = lax.all_to_all(grad_att.reshape(S, U, H, W).transpose(0, 2, 1, 3), "h", 1, 1)
+    dq, dk, dv = attend_back(inv, q_scaled, k_all, v_all, g_att.reshape(-1, W), att, lse)
+    dkv = jnp.stack([dk, dv]).reshape(2, npair, 2, U, W)
+    dkv = dkv[:, :, 0] + from_other(dkv[:, :, 1])
+    dkv = dkv.reshape(2, -1, W).astype(bf16)
+    grad_mixed = jnp.concatenate([dq, dkv[0], dkv[1]], axis=1)
+    grad_qkv = jnp.dot(normed.T, grad_mixed, preferred_element_type=f32)
+    cols = jnp.sum(grad_mixed.astype(f32), axis=0)
+    t = jnp.dot(grad_mixed, w_h.T, preferred_element_type=f32)
+    t = lax.psum_scatter(t.reshape(S, H, U, D), "h", scatter_dimension=1, tiled=False)
+    _, norm_back_one = jax.vjp(layer_norm, x_own, g1, b1)
+    grad_inputs, grad_g1, grad_b1 = norm_back_one(t.reshape(rows, D))
+    grad_hidden = (grad_inputs + grad_middle).astype(bf16)
+    back = lambda y: lax.all_to_all(y.reshape(S, U, D), "s", 0, 0).reshape(rows, D)
+
+    gq = grad_qkv.reshape(S, H, Q, d, 3 * W)
+    gq = lax.psum_scatter(lax.psum_scatter(gq, "s", scatter_dimension=0, tiled=False), "r", scatter_dimension=1, tiled=False)
+    gq = lax.all_to_all(gq, "h", 0, 0)
+    gq = gq.reshape(H, d, 3, W).transpose(1, 2, 0, 3).reshape(d, 3 * D)
+    place = lambda c: lax.dynamic_update_slice_in_dim(jnp.zeros((D,), f32), c, h * W, 0)
+    small = [grad_g1, grad_b1, place(cols[:W]), place(cols[2 * W :]), grad_bout, grad_g2, grad_b2, grad_bproj, grad_bfc]
+    scat = lambda y: lax.psum_scatter(y, AXES, scatter_dimension=0, tiled=True)
+    g1s, b1s, bqs, bvs, bos, g2s, b2s, bps, bfs = [scat(y) for y in small]
+    return (
+        back(layer_out),
+        back(grad_hidden),
+        g1s,
+        b1s,
+        gq,
+        bqs,
+        bvs,
+        scat(grad_wout),
+        bos,
+        g2s,
+        b2s,
+        scat(grad_fc),
+        bfs,
+        scat(grad_proj),
+        bps,
+    )
+
+
+def solution(mesh):
+    n = mesh.shape["ctx"]
+    if n // (PLANES * SEQS) != 2:
+        return solution_any(mesh)
+    split = Mesh(mesh.devices.reshape(PLANES, SEQS, -1), AXES)
+    row, vec = P(AXES, None), P(AXES)
+    return jax.shard_map(
+        planes,
+        mesh=split,
+        in_specs=(row, P(), vec, vec, row, vec, vec, row, vec, vec, vec, row, vec, row, vec, row),
+        out_specs=(row, row, vec, vec, row, vec, vec, row, vec, vec, vec, row, vec, row, vec),
+        check_vma=False,
+    )

time: 1430 us -> 1020 us (0.71)
  matrix products: 412 us -> 68.8 us
  local copies, waits for them, and re-layouts: 362 us -> 66.9 us
  waiting for transfers between devices: 328 us -> 536 us
  Pallas kernels: 0 us -> 107 us
  other arithmetic: 122 us -> 40.9 us
  blocking collectives: 178 us -> 147 us
  starting transfers between devices: 1.95 us -> 26.8 us
    dot_general x47 -> x12, matrix products: 412 us -> 68.8 us  [the longest x1 10.3 us: planes(): grad_proj = jnp.dot(activation.T, g_own, preferred_element_type=f32)]
    reduce_scatter x4, waiting for transfers between devices: 67.3 us -> 357 us  [the longest x3 317 us: planes(): scat = lambda y: lax.psum_scatter(y, AXES, scatter_dimension=0, tiled=True)]
    all_gather x8 -> x4, waiting for transfers between devices: 258 us -> 37.7 us  [the longest x3 37.7 us: planes(): gather = lambda x: lax.all_gather(x, AXES, axis=0, tiled=True)]
    dynamic_slice x21 -> x2, local copies, waits for them, and re-layouts: 200 us -> 0.15 us  [the longest x1 0.08 us: planes(): bv_h = lax.dynamic_slice_in_dim(bv, h * W, W)]
    unnamed x12, waiting for transfers between devices: 3.07 us -> 118 us
    pallas_call x0 -> x2, Pallas kernels: none -> 107 us  [the longest x1 54.7 us: attend_back(): pl.pallas_call(attend_back_kernel, grid_spec=pltpu.PrefetchScalarGridSpec...]
    while x59 -> x0, local copies, waits for them, and re-layouts: 79.5 us -> none  [the longest x7 70.1 us: group_loop(): return lax.fori_loop(0, turn_count, one_turn, carried)]
    reduce_sum x27 -> x4, other arithmetic: 83.1 us -> 5.95 us  [the longest x1 2.58 us: planes(): cols = jnp.sum(grad_mixed.astype(f32), axis=0)]
  transfers between devices with their start and end apart: 16 -> 19, of which waited for: 4 -> 9; matrix products, arithmetic and copies ran while one was open for 61% -> 11% of each run, Pallas kernels for 0% -> 5%
where the time goes in v1:
time: 1020 us; the launch traced here: 1010 us
  waiting for transfers between devices  536 us (53%)
  blocking collectives  147 us (14%)
  Pallas kernels  107 us (10%)
  matrix products  68.8 us (7%)
  local copies, waits for them, and re-layouts  66.9 us (7%)
  other arithmetic  40.9 us (4%)
  starting transfers between devices  26.8 us (3%)
  between operations  15.3 us (2%)
    reduce_scatter x3, waiting for transfers between devices, planes(): scat = lambda y: lax.psum_scatter(y, AXES, scatter_dimension=0, tiled=True)  317 us
    unnamed x12, waiting for transfers between devices  118 us
    unnamed x2, blocking collectives  80.8 us
    pallas_call x1, Pallas kernels, attend_back(): pl.pallas_call(attend_back_kernel, grid_spec=pltpu.PrefetchScalarGridSpec...  54.7 us
    pallas_call x1, Pallas kernels, attend(): pl.pallas_call(attend_kernel, grid_spec=pltpu.PrefetchScalarGridSpec(num_...  52.5 us
    reduce_scatter x1, waiting for transfers between devices, planes(): lax.psum_scatter(gq, 's', scatter_dimension=0, tiled=False)  39.3 us
    all_gather x3, waiting for transfers between devices, planes(): gather = lambda x: lax.all_gather(x, AXES, axis=0, tiled=True)  37.7 us
    all_to_all x1, blocking collectives, planes(): x_own = lax.all_to_all(hidden_in.reshape(S, U, D), 's', 0, 0)  26.7 us
  transfers between devices with their start and end apart: 19, of which 9 were waited for; matrix products, arithmetic and copies ran while one was open for 11% of the time, Pallas kernels for 5%

profile of v1, /device:TPU:0, one launch (start us, length us, event | category | flops | bytes accessed | tf_op | source)
XLA Modules:
  0.0 1008.9 jit_solution(5258327685078539919)
XLA Ops:
  7.3 26.7 %all_to_all.40 = bf16[4,128,768]{2,1,0:T(8,128)(2,1)} all-to-all(bf16[4,128,768]{2,1,0:T(8,128)(2,1)} %bitcast.185), channel_id=1, replica_groups=mesh['s'=4,'h'=4,'r'=2] {'s'}, dimensions={0} | all-to-all | bytes 1572864 | tf_op jit(solution)/shard_map/all_to_all | solution.py:763
  38.1 3.7 all-to-all-start.1
  42.2 39.9 %all-reduce = bf16[9216]{0:T(1024)(128)(2,1)S(1)} all-reduce(bf16[9216]{0:T(1024)(128)(2,1)S(1)} %dynamic-update-slice), channel_id=3, replica_groups=mesh['s'=4,'h'=4,'r'=2] {'s','h','r'}, use_global_device_ids=true, to_apply=%add | all-reduce | flops 9216 | bytes 36864
  84.9 21.5 %all-gather.3 = bf16[16,2,24,576]{3,2,1,0:T(8,128)(2,1)} all-gather(bf16[4,2,24,576]{3,2,1,0:T(8,128)(2,1)S(1)} %bitcast.182), channel_id=5, replica_groups=mesh['s'=4,'h'=4,'r'=2] {'s'}, dimensions={0}, use_global_device_ids=true | all-gather | bytes 1105920 | tf_op jit(solution)/shard_map/all_gather | solution.py:753
  106.4 2.6 convert_reduce_fusion.3
  122.0 2.8 copy.130
  124.8 2.8 fusion.40.q_ref
  132.1 3.4 pad_maximum_fusion.3
  137.3 52.5 %attend.1 = (f32[2048,192]{1,0:T(8,128)}, f32[8,2048]{1,0:T(8,128)}) custom-call(s32[16]{0:T(128)} %select_reduce_fusion.inv, bf16[2048,192]{1,0:T(8,128)(2,1)} %fusion.40.q_ref, bf16[4096,192]{1,0:T(8,128)(2,1)} %bitcast.159, bf16[4096,192]{1,0:T(8,128)(2,1)} %bitcast.157), custom_call_target="tpu_custom_call" | custom-call | tf_op jit(solution)/shard_map/attend/pallas_call | solution.py:556
  189.8 2.7 convert_element_type.180
  194.8 4.2 all-to-all-start.2
  199.4 11.6 %all-to-all-done.2 = bf16[4,4,128,192]{2,0,3,1:T(4,128)(2,1)} async-done(((bf16[4,4,128,192]{2,0,3,1:T(4,128)(2,1)}), bf16[4,4,128,192]{2,0,3,1:T(4,128)(2,1)}, u32[]{:S(2)}, u32[]{:S(2)}) %all-to-all-start.2) | async-done | bytes 786464 | tf_op jit(solution)/shard_map/all_to_all | solution.py:787
  211.0 4.2 all-to-all-start.4
  215.7 2.7 fusion.62
  219.9 8.1 fusion.55
  228.0 9.8 all-to-all-done.4
  237.8 37.6 %all-gather.13.cloned.1.call-done = bf16[3072,768]{1,0:T(8,128)(2,1)} async-done(((bf16[96,768]{1,0:T(8,128)(2,1)}), bf16[3072,768]{1,0:T(8,128)(2,1)}) %all-gather.13.cloned.1.call-update) | async-done | bytes 4718608 | tf_op jit(solution)/shard_map/all_gather | solution.py:741
  275.4 9.2 convert_reduce_fusion
  284.7 3.0 multiply_reduce_fusion.1
  295.9 2.4 reshape.400
  298.3 16.5 %all_to_all.41 = bf16[4,4,128,192]{2,0,3,1:T(4,128)(2,1)} all-to-all(bf16[4,4,128,192]{2,0,3,1:T(4,128)(2,1)} %bitcast.179), channel_id=1, replica_groups=mesh['s'=4,'h'=4,'r'=2] {'h'}, dimensions={1} | all-to-all | bytes 1572864 | tf_op jit(solution)/shard_map/all_to_all | solution.py:812
  314.8 2.3 copy.107
  317.1 54.7 %attend_back.1 = (bf16[2048,192]{1,0:T(8,128)(2,1)}, f32[4096,192]{1,0:T(8,128)}, f32[4096,192]{1,0:T(8,128)}) custom-call(s32[16]{0:T(128)} %select_reduce_fusion.inv, bf16[2048,192]{1,0:T(8,128)(2,1)} %fusion.40.q_ref, bf16[4096,192]{1,0:T(8,128)(2,1)} %bitcast.160, bf16[4096,192]{1,0:T(8,128)(2,1)} %bitcast.158, bf16[2048,192]{1,0:T(8,128)(2,1)} %bitcast.162, ...), custom_call_target="tpu_custom_call" | custom-call | tf_op jit(solution)/shard_map/attend_back/pallas_call | solution.py:646
  371.8 5.2 copy.108
  377.0 5.2 copy.109
  382.2 3.9 fusion.15
  386.1 2.5 fusion.10
  388.7 4.9 copy.113
  393.6 2.8 fusion.14
  400.0 6.3 fusion.16
  407.1 39.3 %reduce-scatter.9.cloned.1.call-done = f32[1,4,2,24,576]{4,3,2,1,0:T(8,128)} async-done(((f32[4,4,2,24,576]{4,3,2,1,0:T(8,128)}), f32[1,4,2,24,576]{4,3,2,1,0:T(8,128)}) %reduce-scatter.9.cloned.1.call-update) | async-done | bytes 442384 | tf_op jit(solution)/shard_map/reduce_scatter | solution.py:828
  446.5 5.9 fusion.18
  453.5 3.4 fusion.42
  457.2 10.3 %fusion.56 = f32[3072,768]{1,0:T(8,128)} fusion(bf16[512,768]{1,0:T(8,128)(2,1)} %bitcast.18, f32[512,3072]{1,0:T(8,128)} %fusion.55, f32[3072]{0:T(1024)S(1)} %reshape.414), kind=kOutput, calls=%fused_computation.124 | convolution fusion | flops 2431647744 | bytes 16527360 | tf_op jit(solution)/shard_map/dot_general | solution.py:796
  468.9 7.1 fusion.54
  478.2 9.0 add_convert_fusion.2
  487.2 4.2 all-to-all-start.3
  491.4 2.3 dynamic-slice_bitcast_fusion
  493.8 115.8 %all-reduce.16.cloned.1.call-done = f32[4,4,128,768]{3,2,1,0:T(8,128)} async-done(((f32[4,4,128,768]{3,2,1,0:T(8,128)}), f32[4,4,128,768]{3,2,1,0:T(8,128)}) %all-reduce.16.cloned.1.call-update) | async-done | bytes 6291472
  609.5 2.6 fusion.37
  612.9 4.0 all-to-all-start.7
  617.0 3.4 fusion.26
  622.5 4.9 all-to-all-start.6
  628.7 2.6 convert_reduce_fusion.1
  634.1 41.0 %all-reduce.12 = (f32[768]{0:T(1024)S(1)}, f32[768]{0:T(1024)S(1)}, f32[768]{0:T(1024)S(1)}, f32[768]{0:T(1024)S(1)}, f32[768]{0:T(1024)S(1)}, /*index=5*/f32[76...) all-reduce(f32[768]{0:T(1024)S(1)} %get-tuple-element.29, ...), channel_id=7, replica_groups=mesh['s'=4,'h'=4,'r'=2] {'s','h','r'}, use_global_device_ids=true, to_apply=%region_13.14.clone | all-reduce | flops 9216 | bytes 73728
  680.3 34.2 %reduce-scatter.11.cloned.1.call-done = f32[24,768]{1,0:T(8,128)} async-done(((f32[768,768]{1,0:T(8,128)}), f32[24,768]{1,0:T(8,128)}) %reduce-scatter.11.cloned.1.call-update) | async-done | bytes 73744 | tf_op jit(solution)/shard_map/reduce_scatter | solution.py:833
  714.5 142.1 %reduce-scatter.15.cloned.1.call-done = f32[96,768]{1,0:T(8,128)} async-done(((f32[3072,768]{1,0:T(8,128)}), f32[96,768]{1,0:T(8,128)}) %reduce-scatter.15.cloned.1.call-update) | async-done | bytes 294928 | tf_op jit(solution)/shard_map/reduce_scatter | solution.py:833
  856.6 140.9 %reduce-scatter.13.cloned.1.call-done = f32[24,3072]{1,0:T(8,128)} async-done(((f32[768,3072]{1,0:T(8,128)}), f32[24,3072]{1,0:T(8,128)}) %reduce-scatter.13.cloned.1.call-update) | async-done | bytes 294928 | tf_op jit(solution)/shard_map/reduce_scatter | solution.py:833
  (180 shorter events, 64.8 us)
Async XLA Ops:
  7.2 34.6 %copy-start.25 = (bf16[24]{0:T(256)(128)(2,1)S(1)}, bf16[24]{0:T(256)(128)(2,1)}, u32[]{:S(2)}) copy-start(bf16[24]{0:T(256)(128)(2,1)} %param.30) | copy-start | bytes 148
  7.2 34.6 %copy-start.26 = (bf16[96]{0:T(256)(128)(2,1)S(1)}, bf16[96]{0:T(256)(128)(2,1)}, u32[]{:S(2)}) copy-start(bf16[96]{0:T(256)(128)(2,1)} %param.28) | copy-start | bytes 580
  7.2 34.6 %copy-start.24 = (bf16[24]{0:T(256)(128)(2,1)S(1)}, bf16[24]{0:T(256)(128)(2,1)}, u32[]{:S(2)}) copy-start(bf16[24]{0:T(256)(128)(2,1)} %param.26) | copy-start | bytes 148
  7.2 34.6 %copy-start.23 = (bf16[24]{0:T(256)(128)(2,1)S(1)}, bf16[24]{0:T(256)(128)(2,1)}, u32[]{:S(2)}) copy-start(bf16[24]{0:T(256)(128)(2,1)} %param.25) | copy-start | bytes 148
  7.2 34.6 %copy-start.22 = (bf16[24]{0:T(256)(128)(2,1)S(1)}, bf16[24]{0:T(256)(128)(2,1)}, u32[]{:S(2)}) copy-start(bf16[24]{0:T(256)(128)(2,1)} %param.24) | copy-start | bytes 148
  7.2 34.6 %copy-start.21 = (bf16[24]{0:T(256)(128)(2,1)S(1)}, bf16[24]{0:T(256)(128)(2,1)}, u32[]{:S(2)}) copy-start(bf16[24]{0:T(256)(128)(2,1)} %param.22) | copy-start | bytes 148
  7.2 34.6 %copy-start.20 = (bf16[24]{0:T(256)(128)(2,1)S(1)}, bf16[24]{0:T(256)(128)(2,1)}, u32[]{:S(2)}) copy-start(bf16[24]{0:T(256)(128)(2,1)} %param.21) | copy-start | bytes 148
  7.3 34.6 %copy-start.19 = (bf16[24]{0:T(256)(128)(2,1)S(1)}, bf16[24]{0:T(256)(128)(2,1)}, u32[]{:S(2)}) copy-start(bf16[24]{0:T(256)(128)(2,1)} %param.19) | copy-start | bytes 148
  7.3 34.6 %copy-start.18 = (bf16[24]{0:T(256)(128)(2,1)S(1)}, bf16[24]{0:T(256)(128)(2,1)}, u32[]{:S(2)}) copy-start(bf16[24]{0:T(256)(128)(2,1)} %param.18) | copy-start | bytes 148
  7.3 75.0 %copy-start.29 = (s32[32]{0:T(128)S(1)}, s32[32]{0:T(128)}, u32[]{:S(2)}) copy-start(s32[32]{0:T(128)} %param.17) | copy-start | bytes 388
  7.3 99.1 %all-gather.15.cloned.1.call-start = ((), (), s32[]{:S(2)}) async-start(), calls=%async_computation.19 | async-start | bytes 3932160 | tf_op jit(solution)/shard_map/all_gather | solution.py:764
  34.0 181.7 %all-gather.9.cloned.1.call-start = ((), (), s32[]{:S(2)}) async-start(), calls=%async_computation.12 | async-start | bytes 1216512 | tf_op jit(solution)/shard_map/all_gather | solution.py:741
  34.8 185.1 %all-gather.11.cloned.1.call-start = ((), (), s32[]{:S(2)}) async-start(), calls=%async_computation.13 | async-start | bytes 4866048 | tf_op jit(solution)/shard_map/all_gather | solution.py:741
  35.5 239.9 %all-gather.13.cloned.1.call-start = ((), (), s32[]{:S(2)}) async-start(), calls=%async_computation.14 | async-start | bytes 4866048 | tf_op jit(solution)/shard_map/all_gather | solution.py:741
  38.1 44.8 %all-to-all-start.1 = ((bf16[4,24,576]{2,1,0:T(8,128)(2,1)}), bf16[4,24,576]{2,1,0:T(8,128)(2,1)S(1)}, u32[]{:S(2)}, u32[]{:S(2)}) async-start(bf16[4,24,576]{2,1,0:T(8,128)(2,1)} %reshape.386), calls=%async_computation.1 | async-start | bytes 245760 | tf_op jit(solution)/shard_map/all_to_all | solution.py:752
  106.4 2.9 copy-start
  110.3 1.3 copy-start.17
  116.4 11.2 %collective-permute-start.1 = (bf16[2048,192]{0,1:T(8,128)(2,1)}, bf16[2048,192]{0,1:T(8,128)(2,1)}, u32[]{:S(2)}, u32[]{:S(2)}) collective-permute-start(bf16[2048,192]{0,1:T(8,128)(2,1)} %get-tuple-element.48), channel_id=1, source_target_pairs={{0,1},{1,0},{2,3},{3,2},{4,5},{5,4},{6,7},{7,6},{8,9},{9,8},{10,11... | collective-permute-start | bytes 2359304 | tf_op jit(solution)/shard_map/ppermute | solution.py:778
  116.4 13.4 %collective-permute-start = (bf16[2048,192]{0,1:T(8,128)(2,1)}, bf16[2048,192]{0,1:T(8,128)(2,1)}, u32[]{:S(2)}, u32[]{:S(2)}) collective-permute-start(bf16[2048,192]{0,1:T(8,128)(2,1)} %slice.122), channel_id=1, source_target_pairs={{0,1},{1,0},{2,3},{3,2},{4,5},{5,4},{6,7},{7,6},{8,9},{9,8},{10,11... | collective-permute-start | bytes 2359304 | tf_op jit(solution)/shard_map/ppermute | solution.py:778
  132.1 3.4 copy-start.10
  132.1 3.4 copy-start.11
  194.8 16.2 %all-to-all-start.2 = ((bf16[4,4,128,192]{2,0,3,1:T(4,128)(2,1)}), bf16[4,4,128,192]{2,0,3,1:T(4,128)(2,1)}, u32[]{:S(2)}, u32[]{:S(2)}) async-start(bf16[4,4,128,192]{2,0,3,1:T(4,128)(2,1)} %copy.105), calls=%async_computation.2 | async-start | bytes 1572864 | tf_op jit(solution)/shard_map/all_to_all | solution.py:787
  211.0 26.8 %all-to-all-start.4 = ((bf16[4,128,768]{2,1,0:T(8,128)(2,1)}), bf16[4,128,768]{2,1,0:T(8,128)(2,1)}, u32[]{:S(2)}, u32[]{:S(2)}) async-start(bf16[4,128,768]{2,1,0:T(8,128)(2,1)} %bitcast.186), calls=%async_computation.4 | async-start | bytes 1572864 | tf_op jit(solution)/shard_map/all_to_all | solution.py:765
  215.2 231.2 %reduce-scatter.9.cloned.1.call-start = ((), (), s32[]{:S(2)}) async-start(), calls=%async_computation.15 | async-start | bytes 2457600 | tf_op jit(solution)/shard_map/reduce_scatter | solution.py:828
  218.4 1.1 copy-start.4
  275.4 9.3 copy-start.5
  275.4 9.3 copy-start.27
  284.6 3.0 copy-start.32
  287.7 4.2 copy-start.28
  288.3 1.1 copy-start.3
  386.1 7.5 collective-permute-start.2
  388.7 4.9 copy-start.2
  396.4 3.6 copy-start.7
  398.3 8.1 copy-start.8
  400.0 6.4 copy-start.9
  406.4 40.1 %copy-start.13 = (bf16[1,16,128,192]{2,3,1,0:T(8,128)(2,1)S(1)}, bf16[1,16,128,192]{2,3,1,0:T(8,128)(2,1)}, u32[]{:S(2)}) copy-start(bf16[1,16,128,192]{2,3,1,0:T(8,128)(2,1)} %copy-done.12) | copy-start | bytes 2359300
  406.4 40.1 %copy-start.14 = (bf16[1,16,128,192]{2,3,1,0:T(8,128)(2,1)S(1)}, bf16[1,16,128,192]{2,3,1,0:T(8,128)(2,1)}, u32[]{:S(2)}) copy-start(bf16[1,16,128,192]{2,3,1,0:T(8,128)(2,1)} %get-tuple-element.51) | copy-start | bytes 2359300
  406.4 85.0 %all-reduce.18.cloned.1.call-start = ((), (), s32[]{:S(2)}) async-start(), calls=%async_computation.21 | async-start | bytes 983040
  446.4 163.1 %all-reduce.16.cloned.1.call-start = ((), (), s32[]{:S(2)}) async-start(), calls=%async_computation.20 | async-start | bytes 12582912
  452.4 262.1 %reduce-scatter.11.cloned.1.call-start = ((), (), s32[]{:S(2)}) async-start(), calls=%async_computation.16 | async-start | bytes 2433024 | tf_op jit(solution)/shard_map/reduce_scatter | solution.py:833
  456.9 399.7 %reduce-scatter.15.cloned.1.call-start = ((), (), s32[]{:S(2)}) async-start(), calls=%async_computation.18 | async-start | bytes 9732096 | tf_op jit(solution)/shard_map/reduce_scatter | solution.py:833
  467.5 1.4 copy-start.6
  467.5 530.0 %reduce-scatter.13.cloned.1.call-start = ((), (), s32[]{:S(2)}) async-start(), calls=%async_computation.17 | async-start | bytes 9732096 | tf_op jit(solution)/shard_map/reduce_scatter | solution.py:833
  476.0 1.3 copy-start.30
  476.1 1.9 copy-start.1
  487.2 125.7 %all-to-all-start.3 = ((bf16[4,128,768]{2,1,0:T(8,128)(2,1)}), bf16[4,128,768]{2,1,0:T(8,128)(2,1)}, u32[]{:S(2)}, u32[]{:S(2)}) async-start(bf16[4,128,768]{2,1,0:T(8,128)(2,1)} %bitcast.187), calls=%async_computation.3 | async-start | bytes 1572864 | tf_op jit(solution)/shard_map/all_to_all | solution.py:825
  612.9 9.6 all-to-all-start.7
  622.5 57.8 %all-to-all-start.6 = ((bf16[4,128,768]{2,1,0:T(8,128)(2,1)}), bf16[4,128,768]{2,1,0:T(8,128)(2,1)}, u32[]{:S(2)}, u32[]{:S(2)}) async-start(bf16[4,128,768]{2,1,0:T(8,128)(2,1)} %bitcast.180), calls=%async_computation.6 | async-start | bytes 1572864 | tf_op jit(solution)/shard_map/all_to_all | solution.py:825
  (4 other events, 3.6 us)
Sparse Core Ops, SparseCore 0:
  34.1 44.1 all-gather.14
  81.2 55.5 all-gather.8
  139.7 62.5 all-gather.10
  205.0 70.3 all-gather.12
  406.5 39.8 reduce-scatter.8
  448.6 17.8 all-reduce.17
  469.9 139.6 all-reduce.15
  615.4 99.0 reduce-scatter.10
  722.0 134.5 reduce-scatter.14
  863.0 134.4 reduce-scatter.12

commit v2 on v1

--- a/solution.py
+++ b/solution.py
@@ -714,6 +714,348 @@
 PLANES = 4
 
 
+MESH_IDS = pl.DeviceIdType.MESH
+
+
+class Exchange:
+    def __init__(self, send, recv):
+        self.send, self.recv, self.used, self.open = send, recv, 0, []
+        self.s, self.h, self.r = (lax.axis_index(a) for a in AXES)
+        self.planes = lax.axis_size("s")
+        self.xn = self.h + 1 - 2 * lax.rem(self.h, 2)
+        self.yn = lax.rem(self.h + 2, 4)
+        self.dn = lax.rem(self.xn + 2, 4)
+        self.z = lambda j: lax.rem(self.s + j, self.planes)
+        self.X, self.Y, self.D = ({"h": i} for i in (self.xn, self.yn, self.dn))
+        self.C = {"r": 1 - self.r}
+        self.Z = [None] + [{"s": self.z(j)} for j in range(1, self.planes)]
+
+    def greet(self, peers):
+        barrier = pltpu.get_barrier_semaphore()
+        for peer in peers:
+            pl.semaphore_signal(barrier, inc=1, device_id=peer, device_id_type=MESH_IDS)
+        pl.semaphore_wait(barrier, len(peers))
+
+    def slots(self, count):
+        self.used += count
+        return range(self.used - count, self.used)
+
+    def copy(self, i, src, dst, peer):
+        return pltpu.make_async_remote_copy(
+            src_ref=src,
+            dst_ref=dst,
+            send_sem=self.send.at[i],
+            recv_sem=self.recv.at[i],
+            device_id=peer,
+            device_id_type=MESH_IDS,
+        )
+
+    def put(self, i, src, dst, peer):
+        moved = self.copy(i, src, dst, peer)
+        moved.start()
+        self.open.append(moved)
+
+    def got(self, i, dst):
+        self.copy(i, dst, dst, self.X).wait_recv()
+
+    def close(self):
+        for moved in self.open:
+            moved.wait_send()
+
+
+def spread_kernel(x_ref, g_ref, w_ref, xa_ref, ga_ref, wa_ref, send, recv, local):
+    ex = Exchange(send, recv)
+    s, h, r, n = ex.s, ex.h, ex.r, ex.planes
+    own = [
+        pltpu.make_async_copy(x_ref.at[s], xa_ref.at[s, h], local.at[0]),
+        pltpu.make_async_copy(w_ref.at[h], wa_ref.at[s, h, r], local.at[1]),
+        pltpu.make_async_copy(g_ref.at[s], ga_ref.at[s], local.at[2]),
+    ]
+    for c in own:
+        c.start()
+    ex.greet([ex.X, ex.Y, ex.D, ex.C] + ex.Z[1:])
+    iz, iw, ig = ex.slots(n), ex.slots(4), ex.slots(n)
+    ix, iy, ir = ex.slots(n), ex.slots(n), ex.slots(n)
+    iwz, iwc = ex.slots(n), ex.slots(n)
+    for j in range(1, n):
+        ex.put(iz[j], x_ref.at[ex.z(j)], xa_ref.at[s, h], ex.Z[j])
+    for k, (peer, to) in enumerate(((ex.X, ex.xn), (ex.Y, ex.yn), (ex.D, ex.dn))):
+        ex.put(iw[k], w_ref.at[to], wa_ref.at[s, h, r], peer)
+    own[0].wait()
+
+    def forward(j):
+        t = ex.z(j)
+        ex.put(ix[j], xa_ref.at[t, h], xa_ref.at[t, h], ex.X)
+        ex.put(iy[j], xa_ref.at[t, h], xa_ref.at[t, h], ex.Y)
+
+    def relay(j):
+        t = ex.z(j)
+        if j < n // 2:
+            ex.got(ix[j], xa_ref.at[t, ex.xn])
+            ex.put(ir[j], xa_ref.at[t, ex.xn], xa_ref.at[t, ex.xn], ex.Y)
+        else:
+            ex.got(iy[j], xa_ref.at[t, ex.yn])
+            ex.put(ir[j], xa_ref.at[t, ex.yn], xa_ref.at[t, ex.yn], ex.X)
+
+    forward(0)
+    own[1].wait()
+    for k, frm in enumerate((ex.xn, ex.yn, ex.dn)):
+        ex.got(iw[k], wa_ref.at[s, frm, r])
+    for j in range(1, n):
+        ex.put(iwz[j], wa_ref.at[s, :, r], wa_ref.at[s, :, r], ex.Z[j])
+    ex.put(iwc[0], wa_ref.at[s, :, r], wa_ref.at[s, :, r], ex.C)
+    for j in (1, 3, 2):
+        ex.got(iz[n - j], xa_ref.at[ex.z(j), h])
+        forward(j)
+    for j in range(1, n):
+        ex.put(ig[j], g_ref.at[ex.z(j)], ga_ref.at[s], ex.Z[j])
+    relay(0)
+    for j in range(1, n):
+        t = ex.z(j)
+        ex.got(iwz[n - j], wa_ref.at[t, :, r])
+        ex.put(iwc[j], wa_ref.at[t, :, r], wa_ref.at[t, :, r], ex.C)
+    for j in (1, 3, 2):
+        relay(j)
+    for j in range(n):
+        t = ex.z(j)
+        if j < n // 2:
+            ex.got(iy[j], xa_ref.at[t, ex.yn])
+        else:
+            ex.got(ix[j], xa_ref.at[t, ex.xn])
+        ex.got(ir[j], xa_ref.at[t, ex.dn])
+    for j in range(1, n):
+        ex.got(ig[n - j], ga_ref.at[ex.z(j)])
+    for j in range(n):
+        ex.got(iwc[j], wa_ref.at[ex.z(j), :, 1 - r])
+    own[2].wait()
+    ex.close()
+
+
+def remote_call(kernel, cid, out_shape, in_specs, out_specs, scratch, sems, name, vmem=56 << 20):
+    return pl.pallas_call(
+        kernel,
+        out_shape=out_shape,
+        in_specs=in_specs,
+        out_specs=out_specs,
+        scratch_shapes=scratch
+        + [pltpu.SemaphoreType.DMA((sems,)), pltpu.SemaphoreType.DMA((sems,)), pltpu.SemaphoreType.DMA((8,))],
+        compiler_params=pltpu.CompilerParams(
+            collective_id=cid, has_side_effects=True, vmem_limit_bytes=vmem
+        ),
+        name=name,
+    )
+
+
+ANY = pl.BlockSpec(memory_space=pl.ANY)
+VMEM = pl.BlockSpec(memory_space=pltpu.VMEM)
+
+
+def spread_rows(x, g, w):
+    S, U, D = x.shape
+    H, d, N = w.shape
+    Q = lax.axis_size("r")
+    bf16 = jnp.bfloat16
+    return remote_call(
+        spread_kernel,
+        0,
+        [
+            jax.ShapeDtypeStruct((S, H, U, D), bf16),
+            jax.ShapeDtypeStruct((S, U, D), bf16),
+            jax.ShapeDtypeStruct((S, H, Q, d, N), bf16),
+        ],
+        [ANY] * 3,
+        [ANY] * 3,
+        [],
+        8 * S + 4,
+        "spread",
+    )(x, g, w)
+
+
+def gather_kernel(count, *refs):
+    ins, outs, (send, recv, local) = refs[:count], refs[count : 2 * count], refs[2 * count :]
+    ex = Exchange(send, recv)
+    s, h, r, n = ex.s, ex.h, ex.r, ex.planes
+    own = [pltpu.make_async_copy(a, o.at[s, h, r], local.at[i]) for i, (a, o) in enumerate(zip(ins, outs))]
+    for c in own:
+        c.start()
+    ex.greet([ex.X, ex.Y, ex.C] + ex.Z[1:])
+    iz, ix, iy, ir, ic = ([ex.slots(n) for _ in outs] for _ in range(5))
+    for j in range(1, n):
+        for k, (a, o) in enumerate(zip(ins, outs)):
+            ex.put(iz[k][j], a, o.at[s, h, r], ex.Z[j])
+    for c in own:
+        c.wait()
+
+    def forward(j):
+        t = ex.z(j)
+        for k, o in enumerate(outs):
+            if j:
+                ex.got(iz[k][n - j], o.at[t, h, r])
+            ex.put(ix[k][j], o.at[t, h, r], o.at[t, h, r], ex.X)
+            ex.put(iy[k][j], o.at[t, h, r], o.at[t, h, r], ex.Y)
+
+    def relay(j):
+        t = ex.z(j)
+        for k, o in enumerate(outs):
+            if j < n // 2:
+                ex.got(ix[k][j], o.at[t, ex.xn, r])
+                ex.put(ir[k][j], o.at[t, ex.xn, r], o.at[t, ex.xn, r], ex.Y)
+            else:
+                ex.got(iy[k][j], o.at[t, ex.yn, r])
+                ex.put(ir[k][j], o.at[t, ex.yn, r], o.at[t, ex.yn, r], ex.X)
+
+    def across(j):
+        t = ex.z(j)
+        for k, o in enumerate(outs):
+            if j < n // 2:
+                ex.got(iy[k][j], o.at[t, ex.yn, r])
+            else:
+                ex.got(ix[k][j], o.at[t, ex.xn, r])
+            ex.got(ir[k][j], o.at[t, ex.dn, r])
+            ex.put(ic[k][j], o.at[t, :, r], o.at[t, :, r], ex.C)
+
+    order = (0, 1, 3, 2)
+    forward(0)
+    for a, b in zip(order, order[1:]):
+        forward(b)
+        relay(a)
+    relay(order[-1])
+    for j in order:
+        across(j)
+    for j in order:
+        for k, o in enumerate(outs):
+            ex.got(ic[k][j], o.at[ex.z(j), :, 1 - r])
+    ex.close()
+
+
+def gather_all(*arrays):
+    S, H, Q = (lax.axis_size(a) for a in AXES)
+    n = len(arrays)
+    return remote_call(
+        partial(gather_kernel, n),
+        1,
+        [jax.ShapeDtypeStruct((S, H, Q) + a.shape, a.dtype) for a in arrays],
+        [ANY] * n,
+        [ANY] * n,
+        [],
+        5 * S * n,
+        "gather_all",
+    )(*arrays)
+
+
+def by_tile(shape, step):
+    height, width = shape
+    if height % 16:
+
+        @pl.loop(0, width // 768)
+        def _(i):
+            step(slice(None), pl.ds(pl.multiple_of(i * 768, 768), 768))
+    else:
+
+        @pl.loop(0, height // 32)
+        def _(i):
+            step(pl.ds(pl.multiple_of(i * 32, 32), 32), slice(None))
+
+
+def reduce_kernel(count, *refs):
+    ins, outs, rest = refs[:count], refs[count : 2 * count], refs[2 * count :]
+    mine, from_c, one, two, from_z = (rest[i * count : (i + 1) * count] for i in range(5))
+    send, recv, local = rest[5 * count :]
+    ex = Exchange(send, recv)
+    s, h, r, n = ex.s, ex.h, ex.r, ex.planes
+    own = [
+        pltpu.make_async_copy(a.at[:, :, r], m, local.at[k]) for k, (a, m) in enumerate(zip(ins, mine))
+    ]
+    for c in own:
+        c.start()
+    ex.greet([ex.X, ex.Y, ex.C] + ex.Z[1:])
+    ic, i1, i2, iz = ([ex.slots(n) for _ in ins] for _ in range(4))
+    i1b = [ex.slots(n) for _ in ins]
+    order = (0, n // 2, 1, n // 2 + 1)
+    for t in order:
+        for k, a in enumerate(ins):
+            ex.put(ic[k][t], a.at[t, :, 1 - r], from_c[k].at[t], ex.C)
+    for c in own:
+        c.wait()
+
+    def add(to, part):
+        def step(rows, cols):
+            to[rows, cols] = (to[rows, cols].astype(jnp.float32) + part[rows, cols].astype(jnp.float32)).astype(to.dtype)
+
+        by_tile(to.shape, step)
+
+    def first(t):
+        peer, near, other = (ex.X, ex.xn, ex.yn) if t < n // 2 else (ex.Y, ex.yn, ex.xn)
+        for k, m in enumerate(mine):
+            ex.got(ic[k][t], from_c[k].at[t])
+            for i, to in ((i1, near), (i1b, ex.dn)):
+                add(m.at[t, to], from_c[k].at[t, to])
+                ex.put(i[k][t], m.at[t, to], one[k].at[t, 0 if i is i1 else 1], peer)
+            for to in (h, other):
+                add(m.at[t, to], from_c[k].at[t, to])
+
+    def second(t):
+        peer, other = (ex.Y, ex.yn) if t < n // 2 else (ex.X, ex.xn)
+        for k, m in enumerate(mine):
+            ex.got(i1b[k][t], one[k].at[t, 1])
+            add(m.at[t, other], one[k].at[t, 1])
+            ex.put(i2[k][t], m.at[t, other], two[k].at[t], peer)
+            ex.got(i1[k][t], one[k].at[t, 0])
+            add(m.at[t, h], one[k].at[t, 0])
+
+    def third(t):
+        for k, m in enumerate(mine):
+            ex.got(i2[k][t], two[k].at[t])
+            add(m.at[t, h], two[k].at[t])
+
+    def far(j):
+        t = ex.z(j)
+        for k, m in enumerate(mine):
+            ex.put(iz[k][j], m.at[t, h], from_z[k].at[j], ex.Z[j])
+
+    for a, b in zip((None,) + order, order + (None,)):
+        if b is not None:
+            first(b)
+        if a is not None:
+            second(a)
+    for t in order:
+        third(t)
+    for j in range(1, n):
+        far(j)
+    for k, (m, o) in enumerate(zip(mine, outs)):
+        for j in range(1, n):
+            ex.got(iz[k][j], from_z[k].at[j])
+
+        def step(rows, cols):
+            total = m[s, h, rows, cols].astype(jnp.float32)
+            for j in range(1, n):
+                total += from_z[k][j, rows, cols].astype(jnp.float32)
+            o[rows, cols] = total
+
+        by_tile(o.shape, step)
+
+    ex.close()
+
+
+def reduce_all(*arrays):
+    S, H, Q = (lax.axis_size(a) for a in AXES)
+    n = len(arrays)
+    tails = [a.shape[3:] for a in arrays]
+    buffers = [
+        [pltpu.VMEM(lead + t, jnp.bfloat16) for t in tails] for lead in ((S, H), (S, H), (S, 2), (S,), (S,))
+    ]
+    return remote_call(
+        partial(reduce_kernel, n),
+        2,
+        [jax.ShapeDtypeStruct(t, jnp.float32) for t in tails],
+        [ANY] * n,
+        [VMEM] * n,
+        sum(buffers, []),
+        5 * S * n,
+        "reduce_all",
+    )(*arrays)
+
+
 def planes(
     hidden_in,
     block_pairs,
@@ -738,20 +1080,26 @@
     rows, D = hidden_in.shape
     U = rows // SEQS
     W = D // H
-    gather = lambda x: lax.all_gather(x, AXES, axis=0, tiled=True)
+    bfn = fc_bias.shape[0]
+    d = qkv_weight.shape[0]
     vectors = [ln1_gain, ln1_bias, query_bias, value_bias, out_bias, ln2_gain, ln2_bias, proj_bias, fc_bias]
     sizes = [v.shape[0] for v in vectors]
-    allv = gather(jnp.concatenate(vectors)[None])
     offs = [sum(sizes[:i]) for i in range(len(sizes))]
+    line = jnp.concatenate(vectors)
+    w4 = qkv_weight.reshape(d, 3, H, W).transpose(2, 0, 1, 3).reshape(H, d, 3 * W)
+    line = jnp.zeros((8, 3 * W), bf16).at[0, : line.shape[0]].set(line)
+    w4 = jnp.concatenate([w4, jnp.broadcast_to(line[None], (H,) + line.shape)], axis=1)
+    x_all, g_own, w_all = spread_rows(hidden_in.reshape(S, U, D), out_grad.reshape(S, U, D), w4)
+    w_all = w_all.reshape(-1, d + 8, 3 * W)
+    w_h = w_all[:, :d].reshape(D, 3 * W)
+    allv = w_all[:, d, : sum(sizes)]
     g1, b1, bq, bv, bo, g2, b2, bp, bf = (
         allv[:, o : o + n].reshape(-1).astype(f32) for o, n in zip(offs, sizes)
     )
-    w_out, w_fc, w_proj = gather(out_weight), gather(fc_weight), gather(proj_weight)
-    d = qkv_weight.shape[0]
-    w4 = qkv_weight.reshape(d, 3, H, W).transpose(2, 0, 1, 3).reshape(H, d, 3 * W)
-    w4 = lax.all_to_all(w4, "h", 0, 0)
-    w4 = lax.all_gather(lax.all_gather(w4, "r", axis=1), "s", axis=0)
-    w_h = w4.reshape(D, 3 * W)
+    pad8 = lambda y: jnp.concatenate([y, jnp.zeros((8, y.shape[1]), y.dtype)])
+    w_fc, w_proj, w_out = gather_all(fc_weight, proj_weight, pad8(out_weight))
+    w_fc, w_proj = w_fc.reshape(D, -1), w_proj.reshape(-1, D)
+    w_out = w_out.reshape(-1, d + 8, D)[:, :d].reshape(D, D)
 
     blk = block_pairs[::2]
     blk = jnp.where(s % 2 == 0, blk, blk.shape[0] - 1 - blk)
@@ -760,10 +1108,9 @@
         jnp.where(blk[None, :] == jnp.arange(npair)[:, None], jnp.arange(npair)[None, :], 0), axis=1
     ).astype(jnp.int32)
 
-    x_own = lax.all_to_all(hidden_in.reshape(S, U, D), "s", 0, 0)
-    x_all = lax.all_gather(x_own, "h", axis=1).reshape(-1, D)
-    g_own = lax.all_to_all(out_grad.reshape(S, U, D), "s", 0, 0).reshape(rows, D)
-    x_own = x_own.reshape(rows, D).astype(f32)
+    x_own = lax.dynamic_index_in_dim(x_all, h, 1, keepdims=False).reshape(rows, D).astype(f32)
+    x_all = x_all.reshape(-1, D)
+    g_own = g_own.reshape(rows, D)
 
     normed = layer_norm(x_all.astype(f32), g1, b1).astype(bf16)
     mixed = jnp.dot(normed, w_h, preferred_element_type=f32)
@@ -829,9 +1176,19 @@
     gq = lax.all_to_all(gq, "h", 0, 0)
     gq = gq.reshape(H, d, 3, W).transpose(1, 2, 0, 3).reshape(d, 3 * D)
     place = lambda c: lax.dynamic_update_slice_in_dim(jnp.zeros((D,), f32), c, h * W, 0)
-    small = [grad_g1, grad_b1, place(cols[:W]), place(cols[2 * W :]), grad_bout, grad_g2, grad_b2, grad_bproj, grad_bfc]
     scat = lambda y: lax.psum_scatter(y, AXES, scatter_dimension=0, tiled=True)
-    g1s, b1s, bqs, bvs, bos, g2s, b2s, bps, bfs = [scat(y) for y in small]
+    early = [grad_bout, grad_g2, grad_b2, grad_bproj]
+    line = jnp.concatenate([y.reshape(-1, d) for y in early] + [grad_bfc.reshape(-1, bfn)], axis=1)
+    line = jnp.concatenate([line, jnp.zeros((line.shape[0], D - line.shape[1]), f32)], axis=1)
+    slab = jnp.concatenate(
+        [grad_wout.reshape(-1, d, D), line[:, None], jnp.zeros((line.shape[0], 7, D), f32)], axis=1
+    )
+    shard = lambda y: y.astype(bf16).reshape((S, H, Q) + y.shape[1:])
+    gfc, gproj, gslab = reduce_all(
+        shard(grad_fc.reshape(S * H * Q, d, -1)), shard(grad_proj.reshape(S * H * Q, -1, D)), shard(slab)
+    )
+    g1s, b1s, bqs, bvs = [scat(y) for y in (grad_g1, grad_b1, place(cols[:W]), place(cols[2 * W :]))]
+    row = gslab[d]
     return (
         back(layer_out),
         back(grad_hidden),
@@ -840,14 +1197,14 @@
         gq,
         bqs,
         bvs,
-        scat(grad_wout),
-        bos,
-        g2s,
-        b2s,
-        scat(grad_fc),
-        bfs,
-        scat(grad_proj),
-        bps,
+        gslab[:d],
+        row[:d],
+        row[d : 2 * d],
+        row[2 * d : 3 * d],
+        gfc,
+        row[4 * d : 4 * d + bfn],
+        gproj,
+        row[3 * d : 4 * d],
     )
 
 

time: 1020 us -> 790 us (0.77)
  waiting for transfers between devices: 536 us -> 165 us
  Pallas kernels: 107 us -> 310 us
  blocking collectives: 147 us -> 72.4 us
  local copies, waits for them, and re-layouts: 66.9 us -> 91.5 us
    reduce_scatter x3 -> x0, waiting for transfers between devices: 317 us -> none  [planes(): scat = lambda y: lax.psum_scatter(y, AXES, scatter_dimension=0, tiled=True)]
    pallas_call x0 -> x3, Pallas kernels: none -> 203 us  [the longest x1 80.4 us: reduce_all(): remote_call(partial(reduce_kernel, n), 2, [jax.ShapeDtypeStruct(t, jnp.fl...]
    all_gather x4 -> x0, waiting for transfers between devices: 37.7 us -> none  [the longest x3 37.7 us: planes(): gather = lambda x: lax.all_gather(x, AXES, axis=0, tiled=True)]
    unnamed x2 -> x1, blocking collectives: 80.8 us -> 45.1 us
    all_to_all x1 -> x0, blocking collectives: 26.7 us -> none  [planes(): x_own = lax.all_to_all(hidden_in.reshape(S, U, D), 's', 0, 0)]
    all_gather x2 -> x0, blocking collectives: 23.5 us -> none  [planes(): w4 = lax.all_gather(lax.all_gather(w4, 'r', axis=1), 's', axis=0)]
    all_to_all x1, waiting for transfers between devices: 11.6 us -> 0.01 us  [planes(): att_low = lax.all_to_all(att.astype(bf16).reshape(S, H, U, W), 'h', 1, 1)]
    all_to_all x1, blocking collectives: 16.5 us -> 27.3 us  [planes(): lax.all_to_all(grad_att.reshape(S, U, H, W).transpose(0, 2, 1, 3), 'h', 1...]
  transfers between devices with their start and end apart: 19 -> 10, of which waited for: 9 -> 3; matrix products, arithmetic and copies ran while one was open for 11% -> 13% of each run, Pallas kernels for 5% -> 19%
where the time goes in v2:
time: 790 us; the launch traced here: 780 us
  Pallas kernels  310 us (39%)
  waiting for transfers between devices  165 us (21%)
  local copies, waits for them, and re-layouts  91.5 us (12%)
  blocking collectives  72.4 us (9%)
  matrix products  63.4 us (8%)
  other arithmetic  45.6 us (6%)
  starting transfers between devices  17.5 us (2%)
  between operations  14.8 us (2%)
    unnamed x5, waiting for transfers between devices  114 us
    pallas_call x1, Pallas kernels, reduce_all(): remote_call(partial(reduce_kernel, n), 2, [jax.ShapeDtypeStruct(t, jnp.fl...  80.4 us
    pallas_call x1, Pallas kernels, gather_all(): remote_call(partial(gather_kernel, n), 1, [jax.ShapeDtypeStruct((S, H, Q)...  69.6 us
    pallas_call x1, Pallas kernels, attend_back(): pl.pallas_call(attend_back_kernel, grid_spec=pltpu.PrefetchScalarGridSpec...  54.7 us
    pallas_call x1, Pallas kernels, spread_rows(): remote_call(spread_kernel, 0, [jax.ShapeDtypeStruct((S, H, U, D), bf16),...  52.7 us
    pallas_call x1, Pallas kernels, attend(): pl.pallas_call(attend_kernel, grid_spec=pltpu.PrefetchScalarGridSpec(num_...  52.5 us
    reduce_scatter x1, waiting for transfers between devices, planes(): lax.psum_scatter(gq, 's', scatter_dimension=0, tiled=False)  49.6 us
    unnamed x1, blocking collectives  45.1 us
  transfers between devices with their start and end apart: 10, of which 3 were waited for; matrix products, arithmetic and copies ran while one was open for 13% of the time, Pallas kernels for 19%

profile of v2, /device:TPU:0, one launch (start us, length us, event | category | flops | bytes accessed | tf_op | source)
XLA Modules:
  0.0 780.4 jit_solution(4240790971805903832)
XLA Ops:
  7.2 6.1 concatenate.50
  15.3 52.7 %spread.1 = (bf16[4,4,128,768]{3,2,1,0:T(8,128)(2,1)}, bf16[4,128,768]{2,1,0:T(8,128)(2,1)}, bf16[4,4,2,32,576]{4,3,2,1,0:T(8,128)(2,1)}) custom-call(bf16[4,128,768]{2,1,0:T(8,128)(2,1)} %bitcast.202, bf16[4,128,768]{2,1,0:T(8,128)(2,1)} %bitcast.203, bf16[4,32,576]{2,1,0:T(8,128)(2,1)} %pad_maximum_fusion.5.w_ref), custom_call_target="tpu_custom_call" | custom-call | tf_op jit(solution)/shard_map/spread/pallas_call | solution.py:858
  69.1 2.3 slice.160
  71.7 2.4 convert_reduce_fusion
  81.9 3.6 fusion.37
  90.6 2.9 copy.158
  94.3 2.8 fusion.49.q_ref
  99.3 3.3 pad_maximum_fusion.2
  104.8 3.3 pad_maximum_fusion.3
  108.2 52.5 %attend.1 = (f32[2048,192]{1,0:T(8,128)}, f32[8,2048]{1,0:T(8,128)}) custom-call(s32[16]{0:T(128)} %select_reduce_fusion.inv, bf16[2048,192]{1,0:T(8,128)(2,1)} %fusion.49.q_ref, bf16[4096,192]{1,0:T(8,128)(2,1)} %bitcast.165, bf16[4096,192]{1,0:T(8,128)(2,1)} %bitcast.167), custom_call_target="tpu_custom_call" | custom-call | tf_op jit(solution)/shard_map/attend/pallas_call | solution.py:556
  160.6 2.7 convert_element_type.194
  163.3 2.3 copy.126
  165.6 4.2 all-to-all-start
  170.9 69.6 %gather_all.1 = (bf16[4,4,2,24,3072]{4,3,2,1,0:T(8,128)(2,1)}, bf16[4,4,2,96,768]{4,3,2,1,0:T(8,128)(2,1)}, bf16[4,4,2,32,768]{4,3,2,1,0:T(8,128)(2,1)}) custom-call(bf16[24,3072]{1,0:T(8,128)(2,1)} %refs_0_.1, bf16[96,768]{1,0:T(8,128)(2,1)} %refs_1_.1, bf16[32,768]{1,0:T(8,128)(2,1)} %concatenate.54.refs_2_), custom_call_target="tpu_custom_call" | custom-call | tf_op jit(solution)/shard_map/gather_all/pallas_call | solution.py:934
  240.5 2.4 slice.166
  244.2 2.7 fusion.69
  247.2 8.8 %fusion.14 = (bf16[3072,512]{0,1:T(8,128)(2,1)}, f32[512,3072]{1,0:T(8,128)S(1)}) fusion(f32[3072]{0:T(1024)S(1)} %reshape.519, bf16[768,3072]{1,0:T(8,128)(2,1)} %bitcast.216, f32[512,768]{1,0:T(8,128)S(1)} %get-tuple-element.97, f32[768]{0:T(1024)S(1)} %reshape.518, f32[768]{0:T(1024)S(1)} %reshape.517, f32[512]{0:T(512)S(1)} %fusion.53, ...), kind=kOutput, calls=%fused_computation.17 | convolution fusion | flops 2433613824 | bytes 15751168 | tf_op jit(solution)/shard_map/dot_general | solution.py:1139
  256.1 6.6 fusion.63
  262.7 3.0 multiply_reduce_fusion.1
  270.5 2.3 copy.127
  272.8 2.4 reshape.504
  275.3 27.3 %all_to_all.25 = bf16[4,4,128,192]{2,0,3,1:T(4,128)(2,1)} all-to-all(bf16[4,4,128,192]{2,0,3,1:T(4,128)(2,1)} %bitcast.193), channel_id=1, replica_groups=mesh['s'=4,'h'=4,'r'=2] {'h'}, dimensions={1} | all-to-all | bytes 1572864 | tf_op jit(solution)/shard_map/all_to_all | solution.py:1159
  302.6 2.3 copy.128
  304.9 54.7 %attend_back.1 = (bf16[2048,192]{1,0:T(8,128)(2,1)}, f32[4096,192]{1,0:T(8,128)}, f32[4096,192]{1,0:T(8,128)}) custom-call(s32[16]{0:T(128)} %select_reduce_fusion.inv, bf16[2048,192]{1,0:T(8,128)(2,1)} %fusion.49.q_ref, bf16[4096,192]{1,0:T(8,128)(2,1)} %bitcast.166, bf16[4096,192]{1,0:T(8,128)(2,1)} %bitcast.168, bf16[2048,192]{1,0:T(8,128)(2,1)} %bitcast.174, ...), custom_call_target="tpu_custom_call" | custom-call | tf_op jit(solution)/shard_map/attend_back/pallas_call | solution.py:646
  359.6 5.2 copy.130
  364.8 5.2 copy.129
  370.1 3.8 fusion.23
  373.9 2.4 fusion.18
  376.3 4.8 copy.133
  381.1 3.3 fusion.22
  390.2 6.8 fusion.25
  399.2 49.6 %reduce-scatter.6.cloned.1.call-done = f32[1,4,2,24,576]{4,3,2,1,0:T(8,128)} async-done(((f32[4,4,2,24,576]{4,3,2,1,0:T(8,128)}), f32[1,4,2,24,576]{4,3,2,1,0:T(8,128)}) %reduce-scatter.6.cloned.1.call-update) | async-done | bytes 442384 | tf_op jit(solution)/shard_map/reduce_scatter | solution.py:1175
  448.9 7.2 fusion.27
  461.3 9.5 %add_convert_fusion.2 = bf16[512,768]{1,0:T(8,128)(2,1)} fusion(f32[512,768]{1,0:T(8,128)} %copy-done.5, bf16[3072,768]{1,0:T(8,128)(2,1)} %bitcast.212, f32[512,3072]{1,0:T(8,128)} %copy-done.22, f32[3072]{0:T(1024)S(1)} %reshape.519, f32[768]{0:T(1024)S(1)} %reshape.520), kind=kOutput, calls=%fused_computation.81 | convolution fusion | flops 2432827392 | bytes 13384704 | tf_op jit(solution)/shard_map/dot_general | solution.py:1141
  470.8 4.4 all-to-all-start.1
  475.2 4.6 copy.138
  480.8 3.3 convolution_convert_fusion.2
  484.1 6.9 convolution_convert_fusion.1
  491.0 4.9 convolution_convert_fusion
  495.9 2.3 dynamic-slice_bitcast_fusion
  498.2 113.9 %all-reduce.12.cloned.1.call-done = f32[4,4,128,768]{3,2,1,0:T(8,128)} async-done(((f32[4,4,128,768]{3,2,1,0:T(8,128)}), f32[4,4,128,768]{3,2,1,0:T(8,128)}) %all-reduce.12.cloned.1.call-update) | async-done | bytes 6291472
  612.1 2.8 fusion.43
  616.9 3.4 all-to-all-start.4
  620.3 3.7 fusion.35
  625.8 4.6 all-to-all-start.3
  630.4 2.9 maximum_maximum_fusion.refs_2_
  633.3 80.4 %reduce_all.1 = (f32[24,3072]{1,0:T(8,128)}, f32[96,768]{1,0:T(8,128)}, f32[32,768]{1,0:T(8,128)}) custom-call(bf16[4,4,2,24,3072]{4,3,2,1,0:T(8,128)(2,1)} %bitcast.173, bf16[4,4,2,96,768]{4,3,2,1,0:T(8,128)(2,1)} %bitcast.172, bf16[4,4,2,32,768]{4,3,2,1,0:T(8,128)(2,1)} %maximum_maximum_fusion.refs_2_), custom_call_target="tpu_custom_call" | custom-call | tf_op jit(solution)/shard_map/reduce_all/pallas_call | solution.py:1047
  720.5 45.1 %all-reduce.8 = (f32[768]{0:T(1024)S(1)}, f32[768]{0:T(1024)S(1)}, f32[768]{0:T(1024)S(1)}, f32[768]{0:T(1024)S(1)}) all-reduce(f32[768]{0:T(1024)S(1)} %get-tuple-element.55, f32[768]{0:T(1024)S(1)} %get-tuple-element.61, f32[768]{0:T(1024)S(1)} %slice_dynamic-update-slice_fusion.1, ...), channel_id=3, replica_groups=mesh['s'=4,'h'=4,'r'=2] {'s','h','r'}, use_global_device_ids=true, to_apply=%region_13.14.clone | all-reduce | flops 3072 | bytes 24576
  (160 shorter events, 61.3 us)
Async XLA Ops:
  68.0 6.1 copy-start
  75.1 1.3 copy-start.12
  78.5 2.2 copy-start.10
  81.7 15.4 %collective-permute-start = (bf16[2048,192]{0,1:T(8,128)(2,1)}, bf16[2048,192]{0,1:T(8,128)(2,1)}, u32[]{:S(2)}, u32[]{:S(2)}) collective-permute-start(bf16[2048,192]{0,1:T(8,128)(2,1)} %slice.208), channel_id=1, source_target_pairs={{0,1},{1,0},{2,3},{3,2},{4,5},{5,4},{6,7},{7,6},{8,9},{9,8},{10,11... | collective-permute-start | bytes 2359304 | tf_op jit(solution)/shard_map/ppermute | solution.py:1125
  85.5 5.0 copy-start.17
  85.5 17.1 %collective-permute-start.1 = (bf16[2048,192]{0,1:T(8,128)(2,1)}, bf16[2048,192]{0,1:T(8,128)(2,1)}, u32[]{:S(2)}, u32[]{:S(2)}) collective-permute-start(bf16[2048,192]{0,1:T(8,128)(2,1)} %get-tuple-element.74), channel_id=1, source_target_pairs={{0,1},{1,0},{2,3},{3,2},{4,5},{5,4},{6,7},{7,6},{8,9},{9,8},{10,11... | collective-permute-start | bytes 2359304 | tf_op jit(solution)/shard_map/ppermute | solution.py:1125
  160.6 9.6 %copy-start.16 = (bf16[24,768]{1,0:T(8,128)(2,1)S(1)}, bf16[24,768]{1,0:T(8,128)(2,1)}, u32[]{:S(2)}) copy-start(bf16[24,768]{1,0:T(8,128)(2,1)} %param.25) | copy-start | bytes 110596
  165.6 78.5 %all-to-all-start = ((bf16[4,4,128,192]{2,0,3,1:T(4,128)(2,1)}), bf16[4,4,128,192]{2,0,3,1:T(4,128)(2,1)}, u32[]{:S(2)}, u32[]{:S(2)}) async-start(bf16[4,4,128,192]{2,0,3,1:T(4,128)(2,1)} %copy.126), calls=%async_computation | async-start | bytes 1572864 | tf_op jit(solution)/shard_map/all_to_all | solution.py:1134
  169.8 279.0 %reduce-scatter.6.cloned.1.call-start = ((), (), s32[]{:S(2)}) async-start(), calls=%async_computation.6 | async-start | bytes 2457600 | tf_op jit(solution)/shard_map/reduce_scatter | solution.py:1175
  246.8 18.9 %copy-start.5 = (f32[512,768]{1,0:T(8,128)}, f32[512,768]{1,0:T(8,128)S(1)}, u32[]{:S(2)}) copy-start(f32[512,768]{1,0:T(8,128)S(1)} %get-tuple-element.97) | copy-start | bytes 4718596
  246.8 9.2 %slice-start = ((s8[4718592]{0:T(1024)(128)(4,1)}), s8[4194304]{0:T(1024)(128)(4,1)S(1)}, s32[]{:S(2)}) async-start(s8[4718592]{0:T(1024)(128)(4,1)} %bitcast.213), calls=%async_computation.9 | async-start | bytes 8388608
  247.2 8.9 %copy-start.3 = (bf16[4,128,768]{2,1,0:T(8,128)(2,1)S(1)}, bf16[4,128,768]{2,1,0:T(8,128)(2,1)}, u32[]{:S(2)}) copy-start(bf16[4,128,768]{2,1,0:T(8,128)(2,1)} %get-tuple-element.47) | copy-start | bytes 2359300
  247.2 8.9 %slice-start.1 = ((s8[4718592]{0:T(1024)(128)(4,1)}), s8[524288]{0:T(1024)(128)(4,1)S(1)}, s32[]{:S(2)}) async-start(s8[4718592]{0:T(1024)(128)(4,1)} %bitcast.213), calls=%async_computation.10 | async-start | bytes 1048576
  247.2 15.5 %slice-start.2 = ((s8[4718592]{0:T(1024)(128)(4,1)}), s8[4194304]{0:T(1024)(128)(4,1)S(1)}, s32[]{:S(2)}) async-start(s8[4718592]{0:T(1024)(128)(4,1)} %bitcast.217), calls=%async_computation.11 | async-start | bytes 8388608
  256.0 6.6 copy-start.22
  256.0 6.6 slice-start.3
  262.7 3.0 copy-start.20
  265.7 3.1 copy-start.11
  266.4 1.2 copy-start.1
  267.9 0.9 copy-start.13
  373.9 7.2 collective-permute-start.2
  397.0 98.9 %all-reduce.14.cloned.1.call-start = ((), (), s32[]{:S(2)}) async-start(), calls=%async_computation.8 | async-start | bytes 983040
  448.9 163.2 %all-reduce.12.cloned.1.call-start = ((), (), s32[]{:S(2)}) async-start(), calls=%async_computation.7 | async-start | bytes 12582912
  456.2 1.4 copy-start.19
  456.2 2.0 copy-start.18
  470.8 146.1 %all-to-all-start.1 = ((bf16[4,128,768]{2,1,0:T(8,128)(2,1)}), bf16[4,128,768]{2,1,0:T(8,128)(2,1)}, u32[]{:S(2)}, u32[]{:S(2)}) async-start(bf16[4,128,768]{2,1,0:T(8,128)(2,1)} %bitcast.204), calls=%async_computation.1 | async-start | bytes 1572864 | tf_op jit(solution)/shard_map/all_to_all | solution.py:1172
  480.8 3.3 copy-start.4
  484.1 6.9 copy-start.6
  484.1 6.9 copy-start.21
  614.9 1.2 copy-start.2
  616.9 8.9 %all-to-all-start.4 = ((f32[4,24,576]{2,1,0:T(8,128)}), f32[4,24,576]{2,1,0:T(8,128)S(1)}, u32[]{:S(2)}, u32[]{:S(2)}) async-start(f32[4,24,576]{2,1,0:T(8,128)} %dynamic-slice_bitcast_fusion), calls=%async_computation.5 | async-start | bytes 491520 | tf_op jit(solution)/shard_map/all_to_all | solution.py:1176
  625.8 142.1 %all-to-all-start.3 = ((bf16[4,128,768]{2,1,0:T(8,128)(2,1)}), bf16[4,128,768]{2,1,0:T(8,128)(2,1)}, u32[]{:S(2)}, u32[]{:S(2)}) async-start(bf16[4,128,768]{2,1,0:T(8,128)(2,1)} %bitcast.187), calls=%async_computation.3 | async-start | bytes 1572864 | tf_op jit(solution)/shard_map/all_to_all | solution.py:1172
  633.3 84.6 %copy-start.7 = (bf16[2048,192]{1,0:T(8,128)(2,1)S(1)}, bf16[2048,192]{1,0:T(8,128)(2,1)}, u32[]{:S(2)}) copy-start(bf16[2048,192]{1,0:T(8,128)(2,1)} %get-tuple-element.49) | copy-start | bytes 2359300
  633.3 84.6 %copy-start.8 = (bf16[1,16,128,192]{3,2,1,0:T(8,128)(2,1)S(1)}, bf16[1,16,128,192]{3,2,1,0:T(8,128)(2,1)}, u32[]{:S(2)}) copy-start(bf16[1,16,128,192]{3,2,1,0:T(8,128)(2,1)} %copy.135) | copy-start | bytes 2359300
  633.3 84.6 %copy-start.9 = (bf16[1,16,128,192]{3,2,1,0:T(8,128)(2,1)S(1)}, bf16[1,16,128,192]{3,2,1,0:T(8,128)(2,1)}, u32[]{:S(2)}) copy-start(bf16[1,16,128,192]{3,2,1,0:T(8,128)(2,1)} %copy.134) | copy-start | bytes 2359300
  719.0 53.0 %copy-start.15 = (f32[24,3072]{1,0:T(8,128)S(1)}, f32[24,3072]{1,0:T(8,128)}, u32[]{:S(2)}) copy-start(f32[24,3072]{1,0:T(8,128)} %get-tuple-element.127) | copy-start | bytes 884740
  719.0 53.7 %copy-start.14 = (f32[96,768]{1,0:T(8,128)S(1)}, f32[96,768]{1,0:T(8,128)}, u32[]{:S(2)}) copy-start(f32[96,768]{1,0:T(8,128)} %get-tuple-element.129) | copy-start | bytes 884740
Sparse Core Ops, SparseCore 0:
  397.1 51.7 reduce-scatter.5
  451.2 17.8 all-reduce.13
  472.5 139.6 all-reduce.11

commit v3 on v0

--- a/solution.py
+++ b/solution.py
@@ -5,6 +5,9 @@
 import jax.numpy as jnp
 from jax import lax
 from jax.sharding import PartitionSpec as P
+from jax.experimental import pallas as pl
+from jax.experimental.pallas import tpu as pltpu
+from jax.sharding import Mesh
 
 HEADS = 12
 SEQS = 4
@@ -487,7 +490,7 @@
     )
 
 
-def solution(mesh):
+def solution_any(mesh):
     return jax.shard_map(
         shards,
         mesh=mesh,
@@ -528,3 +531,964 @@
         ),
         check_vma=False,
     )
+
+
+AXES = ("s", "h", "r")
+PLANES = 4
+
+
+MESH_IDS = pl.DeviceIdType.MESH
+
+
+class At:
+    def __init__(self, ref, *index):
+        self.ref, self.index = ref, index
+
+    def now(self):
+        return self.ref.at[self.index]
+
+    def still(self):
+        return self.ref.at[tuple(i if isinstance(i, slice) else 0 for i in self.index)]
+
+
+ALL = slice(None)
+
+
+class Exchange:
+    def __init__(self, send, recv):
+        self.send, self.recv, self.used, self.open = send, recv, 0, []
+        self.s, self.h, self.r = (lax.axis_index(a) for a in AXES)
+        self.planes = lax.axis_size("s")
+        self.xn = self.h + 1 - 2 * lax.rem(self.h, 2)
+        self.yn = lax.rem(self.h + 2, 4)
+        self.dn = lax.rem(self.xn + 2, 4)
+        self.z = lambda j: lax.rem(self.s + j, self.planes)
+        self.X, self.Y, self.D = ({"h": i} for i in (self.xn, self.yn, self.dn))
+        self.C = {"r": 1 - self.r}
+        self.Z = [None] + [{"s": self.z(j)} for j in range(1, self.planes)]
+
+    def greet(self, peers):
+        barrier = pltpu.get_barrier_semaphore()
+        for peer in peers:
+            pl.semaphore_signal(barrier, inc=1, device_id=peer, device_id_type=MESH_IDS)
+        pl.semaphore_wait(barrier, len(peers))
+
+    def slots(self, count):
+        self.used += count
+        return range(self.used - count, self.used)
+
+    def copy(self, i, src, dst, peer):
+        return pltpu.make_async_remote_copy(
+            src_ref=src,
+            dst_ref=dst,
+            send_sem=self.send.at[i],
+            recv_sem=self.recv.at[i],
+            device_id=peer,
+            device_id_type=MESH_IDS,
+        )
+
+    def put(self, i, src, dst, peer):
+        self.copy(i, src.now() if isinstance(src, At) else src, dst, peer).start()
+        self.open.append((i, src))
+
+    def got(self, i, dst):
+        self.copy(i, dst, dst, self.X).wait_recv()
+
+    def close(self):
+        for i, src in self.open:
+            src = src.still() if isinstance(src, At) else src
+            self.copy(i, src, src, self.X).wait_send()
+
+
+def remote_call(kernel, cid, out_shape, in_specs, out_specs, scratch, sems, name, vmem=56 << 20):
+    return pl.pallas_call(
+        kernel,
+        out_shape=out_shape,
+        in_specs=in_specs,
+        out_specs=out_specs,
+        scratch_shapes=scratch
+        + [pltpu.SemaphoreType.DMA((sems,)), pltpu.SemaphoreType.DMA((sems,)), pltpu.SemaphoreType.DMA((8,))],
+        compiler_params=pltpu.CompilerParams(
+            collective_id=cid, has_side_effects=True, vmem_limit_bytes=vmem
+        ),
+        name=name,
+    )
+
+
+ANY = pl.BlockSpec(memory_space=pl.ANY)
+VMEM = pl.BlockSpec(memory_space=pltpu.VMEM)
+
+
+GATHER_ORDER = (2, 0, 1)
+
+
+def by_x(k, j):
+    return (k + j) % 2 == 0
+
+
+def act(plan, steps, m, c, last_tile):
+    for (em, ec), todo in plan.items():
+        if (em == ec) == last_tile:
+
+            @pl.when(m == em if last_tile else (m == em) & (c == ec))
+            def _():
+                for step, k, *js in todo:
+                    for j in js:
+                        steps[step](k, j)
+
+
+def gather_steps(ins, outs, g_ref, ga_ref, send, recv, local):
+    ex = Exchange(send, recv)
+    s, h, r, n = ex.s, ex.h, ex.r, ex.planes
+    own = [pltpu.make_async_copy(a, o.at[s, h, r], local.at[i]) for i, (a, o) in enumerate(zip(ins, outs))]
+    own.append(pltpu.make_async_copy(g_ref.at[s], ga_ref.at[s], local.at[len(ins)]))
+    for c in own:
+        c.start()
+    ex.greet([ex.X, ex.Y, ex.C] + ex.Z[1:])
+    iz, ix, iy, ir, ic = ([ex.slots(n) for _ in outs] for _ in range(5))
+    ig = ex.slots(n)
+    for k in GATHER_ORDER:
+        for j in range(1, n):
+            ex.put(iz[k][j], ins[k], outs[k].at[s, h, r], ex.Z[j])
+    for j in range(1, n):
+        ex.put(ig[j], g_ref.at[ex.z(j)], ga_ref.at[s], ex.Z[j])
+    for c in own:
+        c.wait()
+
+    def forward(k, j):
+        t, o = ex.z(j), outs[k]
+        if j:
+            ex.got(iz[k][n - j], o.at[t, h, r])
+        ex.put(ix[k][j], At(o, t, h, r), o.at[t, h, r], ex.X)
+        ex.put(iy[k][j], At(o, t, h, r), o.at[t, h, r], ex.Y)
+
+    def relay(k, j):
+        t, o = ex.z(j), outs[k]
+        slots, frm, peer = (ix, ex.xn, ex.Y) if by_x(k, j) else (iy, ex.yn, ex.X)
+        ex.got(slots[k][j], o.at[t, frm, r])
+        ex.put(ir[k][j], At(o, t, frm, r), o.at[t, frm, r], peer)
+
+    def across(k, j):
+        t, o = ex.z(j), outs[k]
+        slots, frm = (iy, ex.yn) if by_x(k, j) else (ix, ex.xn)
+        ex.got(slots[k][j], o.at[t, frm, r])
+        ex.got(ir[k][j], o.at[t, ex.dn, r])
+        ex.put(ic[k][j], At(o, t, ALL, r), o.at[t, :, r], ex.C)
+
+    def last():
+        for j in range(n):
+            for k, o in enumerate(outs):
+                ex.got(ic[k][j], o.at[ex.z(j), :, 1 - r])
+        for j in range(1, n):
+            ex.got(ig[n - j], ga_ref.at[ex.z(j)])
+        ex.close()
+
+    for k in GATHER_ORDER:
+        forward(k, 0)
+    return dict(forward=forward, relay=relay, across=across), last
+
+
+def by_tile(shape, step):
+    height, width = shape
+    if height % 16:
+
+        @pl.loop(0, width // 768)
+        def _(i):
+            step(slice(None), pl.ds(pl.multiple_of(i * 768, 768), 768))
+    else:
+
+        @pl.loop(0, height // 32)
+        def _(i):
+            step(pl.ds(pl.multiple_of(i * 32, 32), 32), slice(None))
+
+
+def reduce_steps(ins, outs, bufs, send, recv, local):
+    count = len(ins)
+    mine, from_c, one, two, from_z = (bufs[i * count : (i + 1) * count] for i in range(5))
+    ex = Exchange(send, recv)
+    s, h, r, n = ex.s, ex.h, ex.r, ex.planes
+    own = [
+        pltpu.make_async_copy(a.at[:, :, r], m, local.at[k]) for k, (a, m) in enumerate(zip(ins, mine))
+    ]
+    for c in own:
+        c.start()
+    ex.greet([ex.X, ex.Y, ex.C] + ex.Z[1:])
+    ic, i1, i2, iz = ([ex.slots(n) for _ in ins] for _ in range(4))
+    i1b = [ex.slots(n) for _ in ins]
+    for k in (1, 0, 2):
+        for j in range(n):
+            ex.put(ic[k][j], At(ins[k], ex.z(j), ALL, 1 - r), from_c[k].at[ex.z(j)], ex.C)
+    for c in own:
+        c.wait()
+
+    def add(to, part):
+        def step(rows, cols):
+            to[rows, cols] = (to[rows, cols].astype(jnp.float32) + part[rows, cols].astype(jnp.float32)).astype(to.dtype)
+
+        by_tile(to.shape, step)
+
+    def first(k, j):
+        t, m = ex.z(j), mine[k]
+        peer, near, other = (ex.X, ex.xn, ex.yn) if by_x(k, j) else (ex.Y, ex.yn, ex.xn)
+        ex.got(ic[k][j], from_c[k].at[t])
+        for slots, at, to in ((i1b, 1, ex.dn), (i1, 0, near)):
+            add(m.at[t, to], from_c[k].at[t, to])
+            ex.put(slots[k][j], At(m, t, to), one[k].at[j, at], peer)
+        for to in (h, other):
+            add(m.at[t, to], from_c[k].at[t, to])
+
+    def second(k, j):
+        t, m = ex.z(j), mine[k]
+        peer, other = (ex.Y, ex.yn) if by_x(k, j) else (ex.X, ex.xn)
+        ex.got(i1b[k][j], one[k].at[j, 1])
+        add(m.at[t, other], one[k].at[j, 1])
+        ex.put(i2[k][j], At(m, t, other), two[k].at[j], peer)
+        ex.got(i1[k][j], one[k].at[j, 0])
+        add(m.at[t, h], one[k].at[j, 0])
+
+    def third(k, j):
+        t, m = ex.z(j), mine[k]
+        ex.got(i2[k][j], two[k].at[j])
+        add(m.at[t, h], two[k].at[j])
+        if j:
+            ex.put(iz[k][j], At(m, t, h), from_z[k].at[j], ex.Z[j])
+
+    def last():
+        for k, (m, o) in enumerate(zip(mine, outs)):
+            for j in range(1, n):
+                ex.got(iz[k][j], from_z[k].at[j])
+
+            def step(rows, cols):
+                total = m[s, h, rows, cols].astype(jnp.float32)
+                for j in range(1, n):
+                    total += from_z[k][j, rows, cols].astype(jnp.float32)
+                o[rows, cols] = total
+
+            by_tile(o.shape, step)
+
+        ex.close()
+
+    return ex, dict(first=first, second=second, third=third), last
+
+
+HD = 64
+
+
+GATHER_PLAN = {
+    (2, 0): [("forward", 2, 1, 3, 2)],
+    (3, 0): [("relay", 0, 0), ("relay", 1, 0), ("relay", 2, 0)],
+    (4, 0): [("relay", 2, 1, 3, 2)],
+    (4, 3): [("forward", 0, 1, 3, 2)],
+    (5, 1): [("relay", 0, 1, 3)],
+    (6, 0): [("forward", 1, 1, 3, 2), ("relay", 0, 2)],
+    (6, 3): [("across", 2, 0, 1, 3, 2), ("across", 0, 0, 1, 3)],
+    (7, 0): [("relay", 1, 1, 3, 2)],
+    (7, 3): [("across", 0, 2), ("across", 1, 0)],
+    (7, 7): [("across", 1, 1, 3, 2)],
+}
+
+
+def attend_kernel(count, inv, blk, q_ref, kv_ref, g_ref, *refs):
+    ins, outs = refs[:count], refs[count + 4 : 2 * count + 4]
+    o_ref, low_ref, lse_ref, ga_ref = refs[count : count + 4]
+    qt, ks, vt, os, send, recv, local = refs[2 * count + 4 :]
+    npair, U, W = q_ref.shape
+    nh = W // HD
+    B = kv_ref.shape[1]
+    TQ, TK = 2 * U, 2 * B
+    steps, last = gather_steps(ins, outs, g_ref, ga_ref, send, recv, local)
+
+    @pl.loop(0, npair)
+    def _(i):
+        p = inv[i]
+        qt[:, pl.ds(pl.multiple_of(i * U, U), U)] = q_ref[p].T
+        kv = kv_ref[p]
+        for h in range(nh):
+            ks[h, pl.ds(i * B, B), :] = kv[:, h * HD : (h + 1) * HD]
+        vct = kv[:, W:].T
+        for h in range(nh):
+            vt[h, 0:HD, pl.ds(pl.multiple_of(i * B, B), B)] = vct[h * HD : (h + 1) * HD]
+            vt[h, HD:, pl.ds(pl.multiple_of(i * B, B), B)] = jnp.ones((vt.shape[1] - HD, B), vt.dtype)
+
+    def tile(m, c, carry, masked):
+        out = []
+        for h in range(nh):
+            mx, acc = carry[h]
+            qh = qt[h * HD : (h + 1) * HD, pl.ds(pl.multiple_of(m * TQ, TQ), TQ)]
+            kh = ks[h, pl.ds(pl.multiple_of(c * TK, TK), TK), :]
+            s = jnp.dot(kh, qh, preferred_element_type=jnp.float32)
+            if masked:
+                row = lax.broadcasted_iota(jnp.int32, s.shape, 0)
+                col = lax.broadcasted_iota(jnp.int32, s.shape, 1)
+                s = jnp.where((row >= B) & (col < U), NEG, s)
+            new = jnp.maximum(mx, jnp.max(s, axis=0, keepdims=True))
+            p = jnp.exp(s - new).astype(jnp.bfloat16)
+            vh = vt[h, :, pl.ds(pl.multiple_of(c * TK, TK), TK)]
+            acc = acc * jnp.exp(mx - new) + jnp.dot(vh, p, preferred_element_type=jnp.float32)
+            out.append((new, acc))
+        return tuple(out)
+
+    @pl.loop(0, npair // 2)
+    def _(m):
+        init = tuple(
+            (jnp.full((1, TQ), NEG, jnp.float32), jnp.zeros((vt.shape[1], TQ), jnp.float32)) for _ in range(nh)
+        )
+
+        def step(c, x):
+            x = tile(m, c, x, False)
+            act(GATHER_PLAN, steps, m, c, False)
+            return x
+
+        carry = lax.fori_loop(0, m, step, init)
+        carry = tile(m, m, carry, True)
+        rows = []
+        for h in range(nh):
+            mx, acc = carry[h]
+            tot = acc[HD : HD + 1]
+            rows.append(acc[:HD] / tot)
+            lse_ref[h : h + 1, pl.ds(pl.multiple_of(m * TQ, TQ), TQ)] = mx + jnp.log(tot)
+        os[pl.ds(pl.multiple_of(m * TQ, TQ), TQ), :] = jnp.concatenate(rows, axis=0).T
+        act(GATHER_PLAN, steps, m, m, True)
+
+    @pl.loop(0, npair)
+    def _(p):
+        o = os[pl.ds(blk[p] * U, U), :]
+        o_ref[pl.ds(pl.multiple_of(p * U, U), U), :] = o
+        low_ref[pl.ds(pl.multiple_of(p * U, U), U), :] = o.astype(jnp.bfloat16)
+
+    last()
+
+
+SMEM = pl.BlockSpec(memory_space=pltpu.SMEM)
+
+
+def attend(inv, blk, q, kv, g, *weights):
+    npair, U, W = q.shape
+    R, K = npair * U, npair * kv.shape[1]
+    nh = W // HD
+    S, H, Q = (lax.axis_size(a) for a in AXES)
+    n = len(weights)
+    f32, bf16 = jnp.float32, jnp.bfloat16
+    return remote_call(
+        partial(attend_kernel, n),
+        1,
+        [
+            jax.ShapeDtypeStruct((R, W), f32),
+            jax.ShapeDtypeStruct((R, W), bf16),
+            jax.ShapeDtypeStruct((8, R), f32),
+            jax.ShapeDtypeStruct(g.shape, bf16),
+        ]
+        + [jax.ShapeDtypeStruct((S, H, Q) + a.shape, a.dtype) for a in weights],
+        [SMEM] * 2 + [VMEM] * 2 + [ANY] * (n + 1),
+        [VMEM] * 3 + [ANY] * (n + 1),
+        [
+            pltpu.VMEM((W, R), bf16),
+            pltpu.VMEM((nh, K, HD), bf16),
+            pltpu.VMEM((nh, HD + 16, K), bf16),
+            pltpu.VMEM((R, W), f32),
+        ],
+        5 * S * n + S,
+        "attend",
+    )(inv, blk, q, kv, g, *weights)
+
+
+REDUCE_PLAN = {
+    (7, 2): [("first", 1, 1, 2, 3, 0)],
+    (7, 6): [("first", 0, 1, 2, 3, 0)],
+    (6, 3): [("second", 1, 1, 2, 3, 0)],
+    (6, 4): [("first", 2, 1, 2, 3, 0)],
+    (5, 3): [("third", 1, 1, 2, 3, 0)],
+    (4, 2): [("second", 0, 1, 2, 3, 0)],
+    (4, 3): [("second", 2, 1, 2, 3, 0)],
+    (3, 1): [("third", 0, 1, 2, 3, 0)],
+    (3, 2): [("third", 2, 1, 2, 3, 0)],
+}
+
+
+def attend_back_kernel(count, inv, blk, q_ref, kv_ref, g_ref, o_ref, lse_ref, *refs):
+    ins, gm_ref, outs = refs[:count], refs[count], refs[count + 1 : 2 * count + 1]
+    bufs = refs[2 * count + 1 : 7 * count + 1]
+    qt, gt, qx, gx, ks, vs, kt, delta, dkv, dqs, over, back, send, recv, local = refs[7 * count + 1 :]
+    npair, U, W = q_ref.shape
+    nh = W // HD
+    B = kv_ref.shape[1]
+    TQ, TK = 2 * U, 2 * B
+    f32, bf16 = jnp.float32, jnp.bfloat16
+    ex, steps, last = reduce_steps(ins, outs, bufs, send, recv, local)
+    swap = ex.slots(npair // 2)
+
+    @pl.loop(0, npair)
+    def _(i):
+        p = inv[i]
+        qc = q_ref[p]
+        gc = g_ref[p]
+        oc = o_ref[pl.ds(p * U, U), :]
+        cols = pl.ds(pl.multiple_of(i * U, U), U)
+        qt[:, cols] = qc.T
+        gt[:, cols] = gc.T
+        prod = (oc * gc.astype(f32)).T
+        zero = jnp.zeros((U, HD), bf16)
+        for h in range(nh):
+            delta[h : h + 1, cols] = jnp.sum(prod[h * HD : (h + 1) * HD], axis=0, keepdims=True)
+            qx[h, pl.ds(i * U, U), :] = jnp.concatenate([zero, qc[:, h * HD : (h + 1) * HD]], axis=1)
+            gx[h, pl.ds(i * U, U), :] = jnp.concatenate([gc[:, h * HD : (h + 1) * HD], zero], axis=1)
+        kv = kv_ref[p]
+        kc, vc = kv[:, :W], kv[:, W:]
+        kt[:, pl.ds(pl.multiple_of(i * B, B), B)] = kc.T
+        for h in range(nh):
+            ks[h, pl.ds(i * B, B), :] = kc[:, h * HD : (h + 1) * HD]
+            vs[h, pl.ds(i * B, B), :] = vc[:, h * HD : (h + 1) * HD]
+
+    dkv[...] = jnp.zeros_like(dkv)
+
+    def tile(m, c, carry, masked):
+        out = []
+        qcols = pl.ds(pl.multiple_of(m * TQ, TQ), TQ)
+        krows = pl.ds(pl.multiple_of(c * TK, TK), TK)
+        for h in range(nh):
+            hs = slice(h * HD, (h + 1) * HD)
+            s = jnp.dot(ks[h, krows, :], qt[hs, qcols], preferred_element_type=f32)
+            p = jnp.exp(s - lse_ref[h : h + 1, qcols])
+            if masked:
+                row = lax.broadcasted_iota(jnp.int32, s.shape, 0)
+                col = lax.broadcasted_iota(jnp.int32, s.shape, 1)
+                p = jnp.where((row >= B) & (col < U), 0.0, p)
+            dp = jnp.dot(vs[h, krows, :], gt[hs, qcols], preferred_element_type=f32)
+            ds = (p * (dp - delta[h : h + 1, qcols])).astype(bf16)
+            dkv[h, krows, :] += jnp.dot(
+                p.astype(bf16), gx[h, qcols, :], preferred_element_type=f32
+            ) + jnp.dot(ds, qx[h, qcols, :], preferred_element_type=f32)
+            out.append(carry[h] + jnp.dot(kt[hs, krows], ds, preferred_element_type=f32))
+        return tuple(out)
+
+    def halves(b, half):
+        rows = pl.ds(pl.multiple_of(b * B + half * U, U), U)
+        parts = [dkv[h, rows, :] for h in range(nh)]
+        return jnp.concatenate([x[:, HD:] for x in parts] + [x[:, :HD] for x in parts], axis=1)
+
+    @pl.loop(0, npair // 2)
+    def _(turn):
+        m = npair // 2 - 1 - turn
+        init = tuple(jnp.zeros((HD, TQ), f32) for _ in range(nh))
+
+        def step(c, x):
+            x = tile(m, c, x, False)
+            act(REDUCE_PLAN, steps, m, c, False)
+            return x
+
+        carry = lax.fori_loop(0, m, step, init)
+        carry = tile(m, m, carry, True)
+        dqs[pl.ds(pl.multiple_of(m * TQ, TQ), TQ), :] = (jnp.concatenate(carry, axis=0).T * 0.125).astype(bf16)
+        for k in range(2):
+            over[2 * m + k] = halves(2 * m + k, 1).astype(bf16)
+        ex.copy(swap[0] + m, over.at[pl.ds(2 * m, 2)], back.at[pl.ds(2 * m, 2)], ex.C).start()
+        act(REDUCE_PLAN, steps, m, m, True)
+
+    @pl.loop(0, npair // 2)
+    def _(m):
+        moved = ex.copy(swap[0] + m, over.at[pl.ds(2 * m, 2)], back.at[pl.ds(2 * m, 2)], ex.C)
+        moved.wait_recv()
+        moved.wait_send()
+
+    @pl.loop(0, npair)
+    def _(p):
+        b = blk[p]
+        rows = pl.ds(b * B, U)
+        parts = [dkv[h, rows, :] for h in range(nh)]
+        own = jnp.concatenate([x[:, HD:] for x in parts] + [x[:, :HD] for x in parts], axis=1)
+        own = (own + back[b].astype(f32)).astype(bf16)
+        gm_ref[p] = jnp.concatenate([dqs[pl.ds(b * U, U), :], own], axis=1)
+
+    last()
+
+
+def attend_back(inv, blk, q, kv, g, o, lse, *grads):
+    npair, U, W = q.shape
+    R, K = npair * U, npair * kv.shape[1]
+    nh = W // HD
+    S, H, Q = (lax.axis_size(a) for a in AXES)
+    n = len(grads)
+    f32, bf16 = jnp.float32, jnp.bfloat16
+    tails = [a.shape[3:] for a in grads]
+    buffers = [[pltpu.VMEM(lead + t, bf16) for t in tails] for lead in ((S, H), (S, H), (S, 2), (S,), (S,))]
+    return remote_call(
+        partial(attend_back_kernel, n),
+        2,
+        [jax.ShapeDtypeStruct((npair, R // npair, 3 * W), bf16)] + [jax.ShapeDtypeStruct(t, f32) for t in tails],
+        [SMEM] * 2 + [VMEM] * 5 + [ANY] * n,
+        [VMEM] * (n + 1),
+        sum(buffers, [])
+        + [
+            pltpu.VMEM((W, R), bf16),
+            pltpu.VMEM((W, R), bf16),
+            pltpu.VMEM((nh, R, 2 * HD), bf16),
+            pltpu.VMEM((nh, R, 2 * HD), bf16),
+            pltpu.VMEM((nh, K, HD), bf16),
+            pltpu.VMEM((nh, K, HD), bf16),
+            pltpu.VMEM((W, K), bf16),
+            pltpu.VMEM((8, R), f32),
+            pltpu.VMEM((nh, K, 2 * HD), f32),
+            pltpu.VMEM((R, W), bf16),
+            pltpu.VMEM((npair, R // npair, 2 * W), bf16),
+            pltpu.VMEM((npair, R // npair, 2 * W), bf16),
+        ],
+        5 * S * n + npair // 2,
+        "attend_back",
+        60 << 20,
+    )(inv, blk, q, kv, g, o, lse, *grads)
+
+
+def front_kernel(
+    x_ref, w_ref, v_ref, norm_ref, q_ref, kv_ref, wt_ref, vec_ref, xo_ref,
+    xa, ws, wa, wf, kv_far, send, recv, local,
+):
+    f32, bf16 = jnp.float32, jnp.bfloat16
+    ex = Exchange(send, recv)
+    s, h, r, n = ex.s, ex.h, ex.r, ex.planes
+    H, U, D = xa.shape[1:]
+    d, N = w_ref.shape
+    W = N // 3 // H
+    own = pltpu.make_async_copy(x_ref.at[s], xa.at[s, h], local.at[0])
+    own.start()
+    for k in range(H):
+        ws[k] = jnp.concatenate(
+            [w_ref[:, c * D + k * W : c * D + (k + 1) * W] for c in range(3)] + [v_ref[...]], axis=1
+        )
+    ex.greet([ex.X, ex.Y, ex.D, ex.C] + ex.Z[1:])
+    iw, ix, iy, ir, iz, iwz, iwc, ik = (ex.slots(n) for _ in range(8))
+    for j in range(1, n):
+        ex.put(iz[j], x_ref.at[ex.z(j)], xa.at[s, h], ex.Z[j])
+    for k, (peer, to) in enumerate(((ex.X, ex.xn), (ex.Y, ex.yn), (ex.D, ex.dn))):
+        ex.put(iw[k], ws.at[to], wa.at[s, h, r], peer)
+    wa[s, h, r] = ws[h]
+    own.wait()
+
+    def forward(j):
+        t = ex.z(j)
+        if j:
+            ex.got(iz[n - j], xa.at[t, h])
+        ex.put(ix[j], xa.at[t, h], xa.at[t, h], ex.X)
+        ex.put(iy[j], xa.at[t, h], xa.at[t, h], ex.Y)
+
+    def relay(j):
+        t = ex.z(j)
+        slots, frm, peer = (ix, ex.xn, ex.Y) if by_x(0, j) else (iy, ex.yn, ex.X)
+        ex.got(slots[j], xa.at[t, frm])
+        ex.put(ir[j], xa.at[t, frm], xa.at[t, frm], peer)
+
+    def weights(j):
+        if j:
+            ex.got(iwz[n - j], wa.at[ex.z(j), :, r])
+        ex.put(iwc[j], wa.at[ex.z(j), :, r], wa.at[ex.z(j), :, r], ex.C)
+
+    forward(0)
+    for k, frm in enumerate((ex.xn, ex.yn, ex.dn)):
+        ex.got(iw[k], wa.at[s, frm, r])
+    for j in range(1, n):
+        ex.put(iwz[j], wa.at[s, :, r], wa.at[s, :, r], ex.Z[j])
+    weights(0)
+    relay(0)
+    for a, b in ((1, None), (3, 1), (2, 3)):
+        forward(a)
+        if b is not None:
+            relay(b)
+    for j in (1, 3, 2):
+        weights(j)
+    for j in range(n):
+        ex.got(iwc[j], wa.at[ex.z(j), :, 1 - r])
+    rows = H * 2 * d
+    for t in range(n):
+        block = wa[t].astype(f32).reshape(rows, N // H + 128)
+        wf[t * rows : (t + 1) * rows] = block
+    wt_ref[...] = wf[:, : N // H].T.astype(bf16)
+    vec_ref[...] = wf[:, N // H :].T[:16]
+    w = wf[:, : N // H].astype(bf16)
+    gain, bias = vec_ref[0:1], vec_ref[1:2]
+
+    def mine(row):
+        picked = jnp.zeros((1, W), f32)
+        for k in range(H):
+            picked = jnp.where(h == k, vec_ref[row : row + 1, k * W : (k + 1) * W], picked)
+        return picked
+
+    bq, bv = mine(2), mine(3)
+
+    def batch(j):
+        t = ex.z(j)
+        slots, frm = (iy, ex.yn) if by_x(0, j) else (ix, ex.xn)
+        ex.got(slots[j], xa.at[t, frm])
+        ex.got(ir[j], xa.at[t, ex.dn])
+        x = xa[t].reshape(H * U, D).astype(f32)
+        normed = layer_norm(x, gain, bias).astype(bf16)
+        norm_ref[t] = normed.reshape(H, U, D)
+        mixed = jnp.dot(normed, w, preferred_element_type=f32)
+        q = (mixed[:, :W] + bq).astype(bf16) * jnp.asarray(0.125, bf16)
+        q_ref[t] = q.reshape(H, U, W)
+        kv = jnp.concatenate([mixed[:, W : 2 * W], mixed[:, 2 * W :] + bv], axis=1).astype(bf16)
+        kv_ref[t, :, 0] = kv.reshape(H, U, 2 * W)
+        ex.put(ik[j], kv_ref.at[t, :, 0], kv_far.at[t], ex.C)
+
+    batch(0)
+    relay(2)
+    batch(1)
+    batch(3)
+    batch(2)
+    out = pltpu.make_async_copy(xa.at[:, h], xo_ref, local.at[1])
+    out.start()
+    for j in (0, 1, 3, 2):
+        t = ex.z(j)
+        ex.got(ik[j], kv_far.at[t])
+        kv_ref[t, :, 1] = kv_far[t]
+    out.wait()
+    ex.close()
+
+
+def front(x, w, v):
+    S, U, D = x.shape
+    d, N = w.shape
+    H, Q = (lax.axis_size(a) for a in AXES[1:])
+    W = N // 3 // H
+    f32, bf16 = jnp.float32, jnp.bfloat16
+    return remote_call(
+        front_kernel,
+        0,
+        [
+            jax.ShapeDtypeStruct((S, H, U, D), bf16),
+            jax.ShapeDtypeStruct((S, H, U, W), bf16),
+            jax.ShapeDtypeStruct((S, H, Q, U, 2 * W), bf16),
+            jax.ShapeDtypeStruct((N // H, D), bf16),
+            jax.ShapeDtypeStruct((16, D), f32),
+            jax.ShapeDtypeStruct((S, U, D), bf16),
+        ],
+        [ANY, VMEM, VMEM],
+        [VMEM] * 6,
+        [
+            pltpu.VMEM((S, H, U, D), bf16),
+            pltpu.VMEM((H, d, N // H + 128), bf16),
+            pltpu.VMEM((S, H, Q, d, N // H + 128), bf16),
+            pltpu.VMEM((D, N // H + 128), f32),
+            pltpu.VMEM((S, H, U, 2 * W), bf16),
+        ],
+        8 * S,
+        "front",
+    )(x, w, v)
+
+
+def norm_back(x, t, gain, grad):
+    mean = jnp.mean(x, axis=-1, keepdims=True)
+    center = x - mean
+    rstd = lax.rsqrt(jnp.mean(center * center, axis=-1, keepdims=True) + 1e-05)
+    z = center * rstd
+    e = t * gain
+    inner = e - jnp.mean(e, axis=-1, keepdims=True) - z * jnp.mean(e * z, axis=-1, keepdims=True)
+    return grad + rstd * inner
+
+
+def finish_kernel(
+    gm_ref, wt_ref, norm_ref, x_ref, gmid_ref, gain_ref, small_ref, out_ref,
+    gh_ref, lo_ref, gq_ref, vec_ref,
+    t_ref, one, two, hid, gw, gw_c, gw_z, gw_sum, vec, send, recv, local,
+):
+    f32, bf16 = jnp.float32, jnp.bfloat16
+    ex = Exchange(send, recv)
+    s, h, r, n = ex.s, ex.h, ex.r, ex.planes
+    half = n // 2
+    H, N = gm_ref.shape[1], gm_ref.shape[3]
+    U, D = t_ref.shape[2], t_ref.shape[3]
+    W = N // 3
+    d = gw.shape[3]
+    keep = pltpu.make_async_copy(out_ref.at[s], lo_ref.at[s], local.at[0])
+    keep.start()
+    ex.greet([ex.X, ex.Y, ex.D, ex.C] + ex.Z[1:])
+    i1, i1b, i2, ih, il, ic, iz, iq = (ex.slots(n) for _ in range(8))
+    iv = ex.slots(3 + n)
+    acc = [jnp.zeros((1, D), f32), jnp.zeros((1, D), f32)]
+
+    def product(j0, to):
+        planes = [ex.z(j) for j in range(j0, j0 + half)]
+        g = jnp.concatenate([gm_ref[t, to] for t in planes], axis=0)
+        prod = jnp.dot(g, wt_ref[...], preferred_element_type=f32)
+        for k, t in enumerate(planes):
+            part = prod[k * U : (k + 1) * U]
+            t_ref[t, to] = part.astype(bf16)
+            acc[0] += jnp.sum(part * norm_ref[t, to].astype(f32), axis=0, keepdims=True)
+            acc[1] += jnp.sum(part, axis=0, keepdims=True)
+
+    ways = ((0, ex.X, ex.xn, ex.yn), (half, ex.Y, ex.yn, ex.xn))
+    for j0, peer, near, other in ways:
+        product(j0, ex.dn)
+        for j in range(j0, j0 + half):
+            ex.put(i1b[j], t_ref.at[ex.z(j), ex.dn], one.at[j, 1], peer)
+    for j0, peer, near, other in ways:
+        product(j0, near)
+        for j in range(j0, j0 + half):
+            ex.put(i1[j], t_ref.at[ex.z(j), near], one.at[j, 0], peer)
+    for j in range(1, n):
+        ex.put(il[j], out_ref.at[ex.z(j)], lo_ref.at[s], ex.Z[j])
+    for j0, peer, near, other in ways:
+        product(j0, other)
+        product(j0, h)
+
+    g_all = gm_ref[...].reshape(n * H * U, N)
+    cols = jnp.sum(g_all.astype(f32), axis=0, keepdims=True)
+    lane = lax.broadcasted_iota(jnp.int32, (1, D), 1) // W
+
+    def placed(c):
+        return jnp.where(lane == h, jnp.concatenate([c] * H, axis=1), 0.0)
+
+    vec[0, 0:1] = acc[0]
+    vec[0, 1:2] = acc[1]
+    vec[0, 2:3] = placed(cols[:, :W])
+    vec[0, 3:4] = placed(cols[:, 2 * W :])
+    vec[0, 4:8] = jnp.zeros((4, D), f32)
+    vec[0, 8:] = small_ref[...]
+    ex.put(iv[0], vec.at[0], vec.at[1], ex.C)
+
+    def qkv_rows(t0):
+        width = H * 2 * d
+        nt = norm_ref[:, :, :, t0 * width : (t0 + half) * width].reshape(n * H * U, half * width)
+        part = lax.dot_general(nt, g_all, (((0,), (0,)), ((), ())), preferred_element_type=f32)
+        gw[t0 : t0 + half] = part.reshape(half, H, 2, d, N).astype(bf16)
+        for t in range(t0, t0 + half):
+            ex.put(ic[t], gw.at[t, :, 1 - r], gw_c.at[t], ex.C)
+
+    def relay(j):
+        t = ex.z(j)
+        peer, other = (ex.Y, ex.yn) if j < half else (ex.X, ex.xn)
+        ex.got(i1b[j], one.at[j, 1])
+        t_ref[t, other] = (t_ref[t, other].astype(f32) + one[j, 1].astype(f32)).astype(bf16)
+        ex.put(i2[j], t_ref.at[t, other], two.at[j], peer)
+
+    def done(j):
+        t = ex.z(j)
+        ex.got(i1[j], one.at[j, 0])
+        ex.got(i2[j], two.at[j])
+        total = t_ref[t, h].astype(f32) + one[j, 0].astype(f32) + two[j].astype(f32)
+        hid[t] = norm_back(x_ref[t].astype(f32), total, gain_ref[0:1], gmid_ref[t]).astype(bf16)
+        if j:
+            ex.put(ih[j], hid.at[t], gh_ref.at[s], ex.Z[j])
+
+    def to_plane(j):
+        t = ex.z(j)
+        if j:
+            ex.put(iz[j], gw_c.at[t], gw_z.at[s], ex.Z[j])
+
+    qkv_rows(0)
+    relay(0)
+    relay(half)
+    ex.got(iv[0], vec.at[1])
+    vec[2] = vec[0] + vec[1]
+    ex.put(iv[1], vec.at[2], vec.at[3], ex.X)
+    qkv_rows(half)
+    relay(1)
+    relay(half + 1)
+    for t in range(n):
+        ex.got(ic[t], gw_c.at[t])
+        gw_c[t] = (gw_c[t].astype(f32) + gw[t, :, r].astype(f32)).astype(bf16)
+    for j in range(1, n):
+        ex.put(iz[j], gw_c.at[ex.z(j)], gw_z.at[s], ex.Z[j])
+    ex.got(iv[1], vec.at[3])
+    vec[4] = vec[2] + vec[3]
+    ex.put(iv[2], vec.at[4], vec.at[5], ex.Y)
+    done(1)
+    done(half + 1)
+    ex.got(iv[2], vec.at[5])
+    vec[6] = vec[4] + vec[5]
+    for j in range(1, n):
+        ex.put(iv[2 + j], vec.at[6], vec.at[6 + j], ex.Z[j])
+    done(half)
+    done(0)
+    own = pltpu.make_async_copy(hid.at[s], gh_ref.at[s], local.at[1])
+    own.start()
+    total = gw_c[s].astype(f32)
+    for j in range(1, n):
+        ex.got(iz[n - j], gw_z.at[ex.z(j)])
+        total += gw_z[ex.z(j)].astype(f32)
+    gw_sum[...] = total
+    for k, (peer, to) in enumerate(((ex.X, ex.xn), (ex.Y, ex.yn), (ex.D, ex.dn))):
+        ex.put(iq[k], gw_sum.at[to], gq_ref.at[h], peer)
+    mine = pltpu.make_async_copy(gw_sum.at[h], gq_ref.at[h], local.at[2])
+    mine.start()
+    for j in range(1, n):
+        ex.got(iv[2 + j], vec.at[6 + j])
+    vec_ref[...] = vec[6] + vec[7] + vec[8] + vec[9]
+    for k, frm in enumerate((ex.xn, ex.yn, ex.dn)):
+        ex.got(iq[k], gq_ref.at[frm])
+    for j in range(1, n):
+        ex.got(il[n - j], lo_ref.at[ex.z(j)])
+        ex.got(ih[n - j], gh_ref.at[ex.z(j)])
+    for c in (keep, own, mine):
+        c.wait()
+    ex.close()
+
+
+def finish(gm, wt, norm, x, gmid, gain, small, out):
+    S, H, U, N = gm.shape
+    D = wt.shape[1]
+    Q = lax.axis_size("r")
+    d = D // (S * H * Q)
+    f32, bf16 = jnp.float32, jnp.bfloat16
+    return remote_call(
+        finish_kernel,
+        3,
+        [
+            jax.ShapeDtypeStruct((S, U, D), bf16),
+            jax.ShapeDtypeStruct((S, U, D), bf16),
+            jax.ShapeDtypeStruct((H, d, N), f32),
+            jax.ShapeDtypeStruct((16, D), f32),
+        ],
+        [VMEM] * 7 + [ANY],
+        [ANY, ANY, ANY, VMEM],
+        [
+            pltpu.VMEM((S, H, U, D), bf16),
+            pltpu.VMEM((S, 2, U, D), bf16),
+            pltpu.VMEM((S, U, D), bf16),
+            pltpu.VMEM((S, U, D), bf16),
+            pltpu.VMEM((S, H, Q, d, N), bf16),
+            pltpu.VMEM((S, H, d, N), bf16),
+            pltpu.VMEM((S, H, d, N), bf16),
+            pltpu.VMEM((H, d, N), f32),
+            pltpu.VMEM((10, 16, D), f32),
+        ],
+        9 * S + 3,
+        "finish",
+    )(gm, wt, norm, x, gmid, gain, small, out)
+
+
+def planes(
+    hidden_in,
+    block_pairs,
+    ln1_gain,
+    ln1_bias,
+    qkv_weight,
+    query_bias,
+    value_bias,
+    out_weight,
+    out_bias,
+    ln2_gain,
+    ln2_bias,
+    fc_weight,
+    fc_bias,
+    proj_weight,
+    proj_bias,
+    out_grad,
+):
+    f32, bf16 = jnp.float32, jnp.bfloat16
+    s, h, r = (lax.axis_index(a) for a in AXES)
+    S, H, Q = (lax.axis_size(a) for a in AXES)
+    rows, D = hidden_in.shape
+    U = rows // SEQS
+    W = D // H
+    bfn = fc_bias.shape[0]
+    d = qkv_weight.shape[0]
+    lines = [ln1_gain, ln1_bias, query_bias, value_bias, out_bias, ln2_gain, ln2_bias, proj_bias]
+    lines = jnp.concatenate([jnp.stack(lines), fc_bias.reshape(-1, d)]).T
+    lines = jnp.pad(lines, ((0, 0), (0, 128 - lines.shape[1])))
+    normed, q_all, kv_all, w_t, vecs, x_own = front(hidden_in.reshape(S, U, D), qkv_weight, lines)
+    g1, b1, _, _, bo, g2, b2, bp = (vecs[i] for i in range(8))
+    bf = vecs[8 : 8 + bfn // d].reshape(-1, S * H * Q, d).swapaxes(0, 1).reshape(-1)
+    pad8 = lambda y: jnp.concatenate([y, jnp.zeros((8, y.shape[1]), y.dtype)])
+
+    blk = block_pairs[::2]
+    blk = jnp.where(s % 2 == 0, blk, blk.shape[0] - 1 - blk)
+    blk = blk.astype(jnp.int32)
+    npair = blk.shape[0]
+    inv = jnp.sum(
+        jnp.where(blk[None, :] == jnp.arange(npair)[:, None], jnp.arange(npair)[None, :], 0), axis=1
+    ).astype(jnp.int32)
+
+    x_own = x_own.reshape(rows, D).astype(f32)
+    q_all = q_all.reshape(npair, U, W)
+    kv_all = kv_all.reshape(npair, 2 * U, 2 * W)
+    att, att_low, lse, g_own, w_fc, w_proj, w_out = attend(
+        inv, blk, q_all, kv_all, out_grad.reshape(S, U, D), fc_weight, proj_weight, pad8(out_weight)
+    )
+    g_own = g_own.reshape(rows, D)
+    w_fc, w_proj = w_fc.reshape(D, -1), w_proj.reshape(-1, D)
+    w_out = w_out.reshape(-1, d + 8, D)[:, :d].reshape(D, D)
+    att_low = lax.all_to_all(att_low.reshape(S, H, U, W), "h", 1, 1)
+    att_low = att_low.transpose(0, 2, 1, 3).reshape(rows, D)
+
+    middle = x_own + jnp.dot(att_low, w_out, preferred_element_type=f32) + bo
+    normed_two = layer_norm(middle, g2, b2).astype(bf16)
+    pre_act = jnp.dot(normed_two, w_fc, preferred_element_type=f32) + bf
+    activation = gelu_tanh(pre_act).astype(bf16)
+    layer_out = (middle + jnp.dot(activation, w_proj, preferred_element_type=f32) + bp).astype(bf16)
+    grad_out = g_own.astype(f32)
+    grad_proj = jnp.dot(activation.T, g_own, preferred_element_type=f32)
+    grad_bproj = jnp.sum(grad_out, axis=0)
+    grad_activ = jnp.dot(g_own, w_proj.T, preferred_element_type=f32)
+    _, gelu_back = jax.vjp(gelu_tanh, pre_act)
+    grad_pre = gelu_back(grad_activ)[0].astype(bf16)
+    grad_fc = jnp.dot(normed_two.T, grad_pre, preferred_element_type=f32)
+    grad_bfc = jnp.sum(grad_pre.astype(f32), axis=0)
+    grad_normed_two = jnp.dot(grad_pre, w_fc.T, preferred_element_type=f32)
+    _, norm_back_two = jax.vjp(layer_norm, middle, g2, b2)
+    grad_middle, grad_g2, grad_b2 = norm_back_two(grad_normed_two)
+    grad_middle = grad_middle + grad_out
+    grad_branch = grad_middle.astype(bf16)
+    grad_wout = jnp.dot(att_low.T, grad_branch, preferred_element_type=f32)
+    grad_bout = jnp.sum(grad_branch.astype(f32), axis=0)
+    grad_att = jnp.dot(grad_branch, w_out.T, preferred_element_type=f32).astype(bf16)
+
+    g_att = lax.all_to_all(grad_att.reshape(S, U, H, W).transpose(0, 2, 1, 3), "h", 1, 1)
+    shard = lambda y: y.astype(bf16).reshape((S, H, Q) + y.shape[1:])
+    grad_mixed, gfc, gproj, gout = attend_back(
+        inv,
+        blk,
+        q_all,
+        kv_all,
+        g_att.reshape(npair, U, W),
+        att,
+        lse,
+        shard(grad_fc.reshape(S * H * Q, d, -1)),
+        shard(grad_proj.reshape(S * H * Q, -1, D)),
+        shard(jnp.pad(grad_wout.reshape(-1, d, D), ((0, 0), (0, 8), (0, 0)))),
+    )
+    fc_rows = [grad_bfc.reshape(-1, D)]
+    small = jnp.concatenate([y[None] for y in (grad_bout, grad_g2, grad_b2, grad_bproj)] + fc_rows)
+    grad_hidden, layer_out, gq, vec = finish(
+        grad_mixed.reshape(S, H, U, 3 * W),
+        w_t,
+        normed,
+        x_own.reshape(S, U, D).astype(bf16),
+        grad_middle.reshape(S, U, D),
+        jnp.broadcast_to(g1[None], (8, D)),
+        small,
+        layer_out.reshape(S, U, D),
+    )
+    gq = gq.reshape(H, d, 3, W).transpose(1, 2, 0, 3).reshape(d, 3 * D)
+    index = (s * H + h) * Q + r
+    pick = lambda v: lax.dynamic_slice_in_dim(v, index * d, d)
+    return (
+        layer_out.reshape(rows, D),
+        grad_hidden.reshape(rows, D),
+        pick((vec[0] - b1 * vec[1]) / g1),
+        pick(vec[1]),
+        gq,
+        pick(vec[2]),
+        pick(vec[3]),
+        gout[:d],
+        pick(vec[8]),
+        pick(vec[9]),
+        pick(vec[10]),
+        gfc,
+        lax.dynamic_slice_in_dim(vec[12:].reshape(-1), index * bfn, bfn),
+        gproj,
+        pick(vec[11]),
+    )
+
+
+def solution(mesh):
+    n = mesh.shape["ctx"]
+    if n // (PLANES * SEQS) != 2:
+        return solution_any(mesh)
+    split = Mesh(mesh.devices.reshape(PLANES, SEQS, -1), AXES)
+    row, vec = P(AXES, None), P(AXES)
+    return jax.shard_map(
+        planes,
+        mesh=split,
+        in_specs=(row, P(), vec, vec, row, vec, vec, row, vec, vec, vec, row, vec, row, vec, row),
+        out_specs=(row, row, vec, vec, row, vec, vec, row, vec, vec, vec, row, vec, row, vec),
+        check_vma=False,
+    )

time: 1430 us -> 397 us (0.28)
  matrix products: 412 us -> 40.8 us
  local copies, waits for them, and re-layouts: 362 us -> 37.8 us
  waiting for transfers between devices: 328 us -> 10.1 us
  Pallas kernels: 0 us -> 289 us
  blocking collectives: 178 us -> 0 us
  other arithmetic: 122 us -> 3.02 us
    dot_general x47 -> x9, matrix products: 412 us -> 40.8 us  [the longest x1 6.72 us: planes(): grad_activ = jnp.dot(g_own, w_proj.T, preferred_element_type=f32)]
    pallas_call x0 -> x4, Pallas kernels: none -> 289 us  [the longest x1 89.6 us: attend_back(): remote_call(partial(attend_back_kernel, n), 2, [jax.ShapeDtypeStruct((npa...]
    all_gather x8 -> x0, waiting for transfers between devices: 258 us -> none  [the longest x1 123 us: shards(): lax.all_gather(v_seq, 'ctx', axis=2, tiled=True)]
    dynamic_slice x21 -> x6, local copies, waits for them, and re-layouts: 200 us -> 3.51 us  [the longest x5 2.93 us: planes(): pick = lambda v: lax.dynamic_slice_in_dim(v, index * d, d)]
    all_gather x2 -> x0, blocking collectives: 90.1 us -> none  [the longest x1 47.5 us: shards(): lax.all_gather(jnp.swapaxes(log_total, 2, 3), 'ctx', axis=2, tiled=True)]
    unnamed x2 -> x0, blocking collectives: 88.3 us -> none
    reduce_sum x28 -> x3, other arithmetic: 83.9 us -> 1.08 us  [the longest x1 0.63 us: planes(): jnp.sum(jnp.where(blk[None, :] == jnp.arange(npair)[:, None], jnp.arange(...]
    while x59 -> x0, local copies, waits for them, and re-layouts: 79.5 us -> none  [the longest x7 70.1 us: group_loop(): return lax.fori_loop(0, turn_count, one_turn, carried)]
  transfers between devices with their start and end apart: 16 -> 2, of which waited for: 4 -> 1; matrix products, arithmetic and copies ran while one was open for 61% -> 4% of each run, Pallas kernels for 0% -> 0%
where the time goes in v3:
time: 397 us; the launch traced here: 390 us
  Pallas kernels  289 us (73%)
  matrix products  40.8 us (10%)
  local copies, waits for them, and re-layouts  37.8 us (10%)
  waiting for transfers between devices  10.1 us (3%)
  starting transfers between devices  7.41 us (2%)
    pallas_call x1, Pallas kernels, attend_back(): remote_call(partial(attend_back_kernel, n), 2, [jax.ShapeDtypeStruct((npa...  89.6 us
    pallas_call x1, Pallas kernels, attend(): remote_call(partial(attend_kernel, n), 1, [jax.ShapeDtypeStruct((R, W), f...  87.5 us
    pallas_call x1, Pallas kernels, finish(): remote_call(finish_kernel, 3, [jax.ShapeDtypeStruct((S, U, D), bf16), jax...  61.4 us
    pallas_call x1, Pallas kernels, front(): remote_call(front_kernel, 0, [jax.ShapeDtypeStruct((S, H, U, D), bf16), j...  50.4 us
    all_to_all x1, waiting for transfers between devices, planes(): att_low = lax.all_to_all(att_low.reshape(S, H, U, W), 'h', 1, 1)  10.1 us
  transfers between devices with their start and end apart: 2, of which 1 were waited for; matrix products, arithmetic and copies ran while one was open for 4% of the time, Pallas kernels for 0%

profile of v3, /device:TPU:0, one launch (start us, length us, event | category | flops | bytes accessed | tf_op | source)
XLA Modules:
  0.0 389.6 jit_solution(17219833057314603243)
XLA Ops:
  0.7 0.8 slice.58
  1.4 0.6 select_reduce_fusion.inv
  2.1 0.7 reshape.166
  2.9 0.7 copy.72
  3.6 0.7 copy.73
  4.4 0.7 copy.74
  5.1 0.7 copy.75
  5.9 0.7 copy.76
  6.6 0.7 copy.77
  7.4 0.7 copy.78
  8.1 0.7 copy.79
  9.6 1.4 concatenate.10.refs_2_
  11.0 50.4 %front.1 = (bf16[4,4,128,768]{3,2,1,0:T(8,128)(2,1)}, bf16[4,4,128,192]{3,2,1,0:T(8,128)(2,1)}, bf16[4,4,2,128,384]{4,3,2,1,0:T(8,128)(2,1)}, bf16[576,768]{1,0:...) custom-call(bf16[4,128,768]{2,1,0:T(8,128)(2,1)} %bitcast.108, bf16[24,2304]{1,0:T(8,128)(2,1)} %w_ref.1, ...), custom_call_target="tpu_custom_call" | custom-call | tf_op jit(solution)/shard_map/front/pallas_call | solution.py:1152
  61.4 87.5 %attend.1 = (f32[2048,192]{1,0:T(8,128)}, bf16[2048,192]{1,0:T(8,128)(2,1)}, f32[8,2048]{1,0:T(8,128)}, bf16[4,128,768]{2,1,0:T(8,128)(2,1)}, bf16[4,4,2,24,3072...) custom-call(s32[16]{0:T(128)} %select_reduce_fusion.inv, ...), custom_call_target="tpu_custom_call" | custom-call | tf_op jit(solution)/shard_map/attend/pallas_call | solution.py:872
  149.0 2.4 copy.81
  151.4 3.7 all-to-all-start
  155.1 1.1 slice.77
  156.7 10.1 %all-to-all-done = bf16[4,4,128,192]{2,0,3,1:T(4,128)(2,1)S(1)} async-done(((bf16[4,4,128,192]{2,0,3,1:T(4,128)(2,1)}), bf16[4,4,128,192]{2,0,3,1:T(4,128)(2,1)S(1)}, u32[]{:S(2)}, u32[]{:S(2)}) %all-to-all-start) | async-done | bytes 786464 | tf_op jit(solution)/shard_map/all_to_all | solution.py:1409
  166.8 1.0 copy.92
  167.8 2.9 fusion.36
  171.1 5.8 %fusion.14 = (bf16[3072,512]{0,1:T(8,128)(2,1)}, f32[512,3072]{1,0:T(8,128)S(1)}) fusion(f32[3072]{0:T(1024)S(1)} %add.117, bf16[768,3072]{1,0:T(8,128)(2,1)S(1)} %bitcast.124, f32[512,768]{1,0:T(8,128)S(1)} %get-tuple-element.80, f32[768]{0:T(1024)S(1)} %get-tuple-element.62, f32[768]{0:T(1024)S(1)} %get-tuple-element.63, f32[512]{0:T(512)S(1)} %fusion.18, ...), kind=kOutput, calls=%fused_computation.17 | convolution fusion | flops 2433613824 | bytes 15751168 | tf_op jit(solution)/shard_map/dot_general | solution.py:1414
  176.9 4.9 %add_convert_fusion = bf16[512,768]{1,0:T(8,128)(2,1)} fusion(f32[512,768]{1,0:T(8,128)S(1)} %get-tuple-element.80, bf16[3072,768]{1,0:T(8,128)(2,1)S(1)} %bitcast.128, f32[512,3072]{1,0:T(8,128)S(1)} %get-tuple-element.83, f32[3072]{0:T(1024)S(1)} %add.117, f32[768]{0:T(1024)S(1)} %get-tuple-element.60), kind=kOutput, calls=%fused_computation.26 | convolution fusion | flops 2432827392 | bytes 13384704 | tf_op jit(solution)/shard_map/dot_general | solution.py:1416
  181.9 6.7 %convert_reduce_fusion = (f32[3072]{0:T(1024)S(1)}, bf16[512,3072]{1,0:T(8,128)(2,1)S(1)}) fusion(f32[512,3072]{1,0:T(8,128)S(1)} %get-tuple-element.83, f32[3072]{0:T(1024)S(1)} %add.117, bf16[512,768]{1,0:T(8,128)(2,1)S(1)} %bitcast.98, bf16[3072,768]{1,0:T(8,128)(2,1)S(1)} %bitcast.129), kind=kOutput, calls=%fused_computation.19 | convolution fusion | flops 2452091904 | bytes 14966784 | tf_op jit(solution)/shard_map/dot_general | solution.py:1420
  188.6 3.0 multiply_reduce_fusion
  191.6 0.6 fusion.34
  193.1 3.5 convolution_convert_fusion.3
  196.6 0.8 convolution_convert_fusion.2
  197.4 1.4 pad.11
  198.8 4.7 %copy.85 = bf16[3072,512]{1,0:T(8,128)(2,1)} copy(bf16[3072,512]{0,1:T(8,128)(2,1)} %get-tuple-element.82) | data formatting | bytes 6291456 | tf_op jit(solution)/shard_map/convert_element_type | solution.py:1415
  203.5 1.5 copy.83
  205.0 1.1 reshape.178
  206.1 3.7 all-to-all-start.1
  209.8 6.7 %convolution_convert_fusion.1 = bf16[32,96,768]{2,1,0:T(8,128)(2,1)} fusion(bf16[32,96,512]{2,1,0:T(8,128)(2,1)} %bitcast.95, bf16[512,768,1]{1,0,2:T(8,128)(2,1)S(1)} %bitcast.99), kind=kOutput, calls=%fused_computation.22 | convolution fusion | flops 2418278400 | bytes 8650752 | tf_op jit(solution)/shard_map/dot_general | solution.py:1418
  216.5 0.6 concatenate.11.small_ref
  217.1 6.5 %convolution_convert_fusion = bf16[768,3072]{1,0:T(8,128)(2,1)} fusion(bf16[512,3072]{1,0:T(8,128)(2,1)} %copy-done.12, f32[512,768]{1,0:T(8,128)S(1)} %get-tuple-element.80, f32[768]{0:T(1024)S(1)} %get-tuple-element.62, f32[768]{0:T(1024)S(1)} %get-tuple-element.63, f32[512]{0:T(512)S(1)} %fusion.18, f32[512]{0:T(512)S(1)} %broadcast_multiply_fusion), kind=kOutput, calls=%fused_computation.20 | convolution fusion | flops 2420244480 | bytes 9447424 | tf_op jit(solution)/shard_map/dot_general | solution.py:1423
  223.6 1.4 copy.84
  225.0 89.6 %attend_back.1 = (bf16[16,128,576]{2,1,0:T(8,128)(2,1)}, f32[24,3072]{1,0:T(8,128)}, f32[96,768]{1,0:T(8,128)}, f32[32,768]{1,0:T(8,128)}) custom-call(s32[16]{0:T(128)} %select_reduce_fusion.inv, s32[16]{0:T(128)} %copy-done.11, bf16[16,128,192]{2,1,0:T(8,128)(2,1)} %bitcast.93, bf16[16,256,384]{2,1,0:T(8,128)(2,1)} %bitcast.87, ...), custom_call_target="tpu_custom_call" | custom-call | tf_op jit(solution)/shard_map/attend_back/pallas_call | solution.py:1014
  314.6 0.6 broadcast_in_dim.46.gain_ref
  315.2 61.4 %finish.1 = (bf16[4,128,768]{2,1,0:T(8,128)(2,1)}, bf16[4,128,768]{2,1,0:T(8,128)(2,1)}, f32[4,24,576]{2,1,0:T(8,128)}, f32[16,768]{1,0:T(8,128)}) custom-call(bf16[4,4,128,576]{3,2,1,0:T(8,128)(2,1)} %bitcast.100, bf16[576,768]{1,0:T(8,128)(2,1)} %get-tuple-element.48.wt_ref, bf16[4,4,128,768]{3,2,1,0:T(8,128)(2,1)} %get-tuple-element.49.norm_ref, ...), custom_call_target="tpu_custom_call" | custom-call | tf_op jit(solution)/shard_map/finish/pallas_call | solution.py:1331
  376.6 1.0 fusion.35
  377.6 0.7 slice.75
  379.5 1.1 reshape.190
  380.9 0.9 reshape.191
  381.7 0.6 slice.71
  384.7 2.1 copy.97
  386.8 0.9 copy.98
  387.7 0.7 copy.99
  388.4 0.7 copy.100
  (67 shorter events, 6.2 us)
Async XLA Ops:
  1.4 60.0 %copy-start.11 = (s32[16]{0:T(128)}, s32[16]{0:T(128)S(1)}, u32[]{:S(2)}) copy-start(s32[16]{0:T(128)S(1)} %broadcast_select_fusion.blk) | copy-start | bytes 196
  149.0 6.2 %copy-start.5 = (bf16[4,4,2,32,768]{4,3,2,1,0:T(8,128)(2,1)S(1)}, bf16[4,4,2,32,768]{4,3,2,1,0:T(8,128)(2,1)}, u32[]{:S(2)}) copy-start(bf16[4,4,2,32,768]{4,3,2,1,0:T(8,128)(2,1)} %get-tuple-element.42) | copy-start | bytes 4718596
  149.0 7.3 %copy-start.10 = (f32[16,768]{1,0:T(8,128)S(1)}, f32[16,768]{1,0:T(8,128)}, u32[]{:S(2)}) copy-start(f32[16,768]{1,0:T(8,128)} %get-tuple-element.43) | copy-start | bytes 147460
  149.0 7.5 %copy-start.2 = (bf16[4,128,768]{2,1,0:T(8,128)(2,1)S(1)}, bf16[4,128,768]{2,1,0:T(8,128)(2,1)}, u32[]{:S(2)}) copy-start(bf16[4,128,768]{2,1,0:T(8,128)(2,1)} %get-tuple-element.38) | copy-start | bytes 2359300
  151.4 15.4 %all-to-all-start = ((bf16[4,4,128,192]{2,0,3,1:T(4,128)(2,1)}), bf16[4,4,128,192]{2,0,3,1:T(4,128)(2,1)S(1)}, u32[]{:S(2)}, u32[]{:S(2)}) async-start(bf16[4,4,128,192]{2,0,3,1:T(4,128)(2,1)} %copy.81), calls=%async_computation | async-start | bytes 1572864 | tf_op jit(solution)/shard_map/all_to_all | solution.py:1409
  166.8 4.3 %slice-start = ((s8[4718592]{0:T(1024)(128)(4,1)}), s8[4194304]{0:T(1024)(128)(4,1)S(1)}, s32[]{:S(2)}) async-start(s8[4718592]{0:T(1024)(128)(4,1)} %bitcast.122), calls=%async_computation.2 | async-start | bytes 8388608
  167.8 3.3 slice-start.1
  170.8 6.1 %slice-start.2 = ((s8[4718592]{0:T(1024)(128)(4,1)}), s8[4194304]{0:T(1024)(128)(4,1)S(1)}, s32[]{:S(2)}) async-start(s8[4718592]{0:T(1024)(128)(4,1)} %bitcast.126), calls=%async_computation.4 | async-start | bytes 8388608
  171.1 5.8 %slice-start.3 = ((s8[4718592]{0:T(1024)(128)(4,1)}), s8[524288]{0:T(1024)(128)(4,1)S(1)}, s32[]{:S(2)}) async-start(s8[4718592]{0:T(1024)(128)(4,1)} %bitcast.126), calls=%async_computation.5 | async-start | bytes 1048576
  188.6 3.0 copy-start.12
  191.6 1.1 copy-start.3
  193.0 4.4 %copy-start = (f32[512,768]{1,0:T(8,128)}, f32[512,768]{1,0:T(8,128)S(1)}, u32[]{:S(2)}) copy-start(f32[512,768]{1,0:T(8,128)S(1)} %get-tuple-element.68) | copy-start | bytes 4718596
  193.1 3.5 copy-start.1
  203.5 6.3 %copy-start.4 = (bf16[4,128,768]{2,1,0:T(8,128)(2,1)S(1)}, bf16[4,128,768]{2,1,0:T(8,128)(2,1)}, u32[]{:S(2)}) copy-start(bf16[4,128,768]{2,1,0:T(8,128)(2,1)} %get-tuple-element.38) | copy-start | bytes 2359300
  206.1 17.6 %all-to-all-start.1 = ((bf16[4,4,128,192]{2,0,3,1:T(4,128)(2,1)}), bf16[4,4,128,192]{2,0,3,1:T(4,128)(2,1)S(1)}, u32[]{:S(2)}, u32[]{:S(2)}) async-start(bf16[4,4,128,192]{2,0,3,1:T(4,128)(2,1)} %bitcast.22), calls=%async_computation.1 | async-start | bytes 1572864 | tf_op jit(solution)/shard_map/all_to_all | solution.py:1434
  315.2 66.6 %copy-start.9 = (f32[32,768]{1,0:T(8,128)S(1)}, f32[32,768]{1,0:T(8,128)}, u32[]{:S(2)}) copy-start(f32[32,768]{1,0:T(8,128)} %get-tuple-element.54) | copy-start | bytes 294916
  376.6 10.2 %copy-start.6 = (bf16[4,128,768]{2,1,0:T(8,128)(2,1)S(1)}, bf16[4,128,768]{2,1,0:T(8,128)(2,1)}, u32[]{:S(2)}) copy-start(bf16[4,128,768]{2,1,0:T(8,128)(2,1)} %get-tuple-element.51) | copy-start | bytes 2359300
  376.6 11.1 %copy-start.8 = (f32[24,3072]{1,0:T(8,128)S(1)}, f32[24,3072]{1,0:T(8,128)}, u32[]{:S(2)}) copy-start(f32[24,3072]{1,0:T(8,128)} %get-tuple-element.116) | copy-start | bytes 884740
  376.6 11.8 %copy-start.7 = (f32[96,768]{1,0:T(8,128)S(1)}, f32[96,768]{1,0:T(8,128)}, u32[]{:S(2)}) copy-start(f32[96,768]{1,0:T(8,128)} %get-tuple-element.118) | copy-start | bytes 884740
